TPU v7x, 768 devices: a whole 4x8x12 slice. The times are simulated.
768 devices in a mesh: rep: 96 (over y, z_lo, x), fsdp: 4 (over z_hi), tp: 2 (over core).
Axes of the slice: x: 4, y: 8, z: 12 (z_hi: 4, z_lo: 3; z = z_hi * 3 + z_lo), core: 2. Of those that a mesh axis runs over, the one named last changes fastest.
Arguments:
- grads: bfloat16 [96, 16384, 384], P('rep', 'fsdp', 'tp'), may hold values from -0.609375 to 0.609375
- slot_panels: int32 [768, 2], P('rep'), may hold values from -1 to 31, as said below
- factor_old: float32 [768, 512, 512], P(('rep', 'fsdp'), 'tp'), may hold values from -6 to 6
Outputs:
- factor_new: float32 [768, 512, 512], P(('rep', 'fsdp'), 'tp')
Inputs may be any that keep to these rules, and one draw needn't show every extreme that they name: `slot_panels`: row r names the row panel i and the column panel j (i <= j) of the upper-triangle tile kept in slot r % 2 of owner r // 2, or -1 twice for an empty slot. Each of the 528 tiles stands in exactly one slot; every owner holds 1 tiles or one more, in its first slots.
All inputs are finite; a program needn't handle non-finite values.
Results may differ from a plain program's by a relative error of at most 0.0028.
Values may be sent and summed in bfloat16 or wider, within the bound.
No kernel may reach another device: no remote copies, remote signals or barrier semaphores. Data moves between devices by JAX's collectives and lax.ppermute only.
A program may use at most 64 MiB of HBM per device.

v0:
```python
import jax
import jax.numpy as jnp
from jax import lax
from jax.sharding import PartitionSpec as P

TILE = 512


def pick_panels(panels, ends):
    valid = ends >= 0
    chosen = jnp.take(panels, jnp.maximum(ends, 0), axis=0)
    return jnp.where(valid[..., None, None], chosen, jnp.zeros((), panels.dtype))


def body(grads, slot_panels, factor_old):
    owners_here = lax.axis_size("fsdp")
    fsdp_place = lax.axis_index("fsdp")
    local_block = grads[0]
    rows_here, width = local_block.shape
    summed_block = lax.psum(local_block.astype(jnp.float32), "rep").astype(jnp.bfloat16)
    slot_count = factor_old.shape[0]
    group_lists = slot_panels.reshape(owners_here, slot_count, 2)
    own_lists = lax.dynamic_index_in_dim(group_lists, fsdp_place, 0, keepdims=False)
    whole_rows = lax.all_gather(summed_block, "fsdp", axis=0, tiled=True)
    all_panels = whole_rows.reshape(-1, TILE, width)
    chosen = pick_panels(all_panels, own_lists)
    first_end = chosen[:, 0]
    second_end = chosen[:, 1]
    partial_tiles = jnp.einsum(
        "sac,sbc->sab", first_end, second_end, preferred_element_type=jnp.float32
    )
    product = lax.psum_scatter(partial_tiles, "tp", scatter_dimension=1, tiled=True)
    return 0.9 * factor_old + 0.1 * product


def solution(mesh):
    placed = (P("rep", "fsdp", "tp"), P("rep", None), P(("rep", "fsdp"), "tp", None))
    return jax.shard_map(
        body, mesh=mesh, in_specs=placed, out_specs=P(("rep", "fsdp"), "tp", None), check_vma=False
    )
```

profile of v0, /device:TPU:1, one launch (start us, length us, event | category | flops | bytes accessed | tf_op | source)
XLA Modules:
  0.0 826.3 jit_solution(225255635410719067)
XLA Ops:
  6.5 0.0 all-gather.2.cloned.1.call-start
  6.5 1.7 bitcast_convert_fusion
  8.3 0.0 copy-start.1
  8.3 459.3 %all-reduce.1 = bf16[4096,192]{0,1:T(8,128)(2,1)} all-reduce(f32[4096,192]{0,1:T(8,128)S(1)} %bitcast_convert_fusion), channel_id=1, replica_groups=mesh['rep'=96,'fsdp'=4,'tp'=2] {'rep'}, use_global_device_ids=true, to_apply=%region_0.0 | all-reduce | flops 786432 | bytes 4718592 | tf_op jit(solution)/shard_map/psum | solution.py:20
  467.6 0.0 all-gather.2.cloned.1.call-update
  467.6 0.0 reduce-scatter.2.cloned.1.call-start
  467.6 0.0 copy-done.1
  467.7 0.1 copy.27
  467.8 0.1 reshape.42
  467.8 0.1 copy.24
  467.9 0.1 copy.23
  468.1 272.4 %all-gather.2.cloned.1.call-done = bf16[16384,192]{0,1:T(8,128)(2,1)} async-done(((bf16[4096,192]{0,1:T(8,128)(2,1)}), bf16[16384,192]{0,1:T(8,128)(2,1)}) %all-gather.2.cloned.1.call-update) | async-done | bytes 6291472 | tf_op jit(solution)/shard_map/all_gather | solution.py:24
  740.4 6.3 copy.33
  746.7 3.4 gather_fusion
  750.1 0.0 copy-start
  750.1 0.2 fusion
  750.3 1.8 fusion.1
  752.1 0.0 reduce-scatter.2.cloned.1.call-update
  752.1 64.9 %reduce-scatter.2.cloned.1.call-done = f32[2,256,512]{2,1,0:T(8,128)} async-done(((f32[2,512,512]{2,1,0:T(8,128)}), f32[2,256,512]{2,1,0:T(8,128)}) %reduce-scatter.2.cloned.1.call-update) | async-done | bytes 1048592 | tf_op jit(solution)/shard_map/reduce_scatter | solution.py:32
  817.1 0.0 copy-done
  817.1 2.4 multiply_add_fusion
  (2 shorter events, 0.0 us)
Async XLA Ops:
  6.5 733.9 %all-gather.2.cloned.1.call-start = ((), (), s32[]{:S(2)}) async-start(), calls=%async_computation.1 | async-start | bytes 7864320 | tf_op jit(solution)/shard_map/all_gather | solution.py:24
  8.3 459.4 %copy-start.1 = (s32[8,2]{0,1:T(2,128)S(1)}, s32[8,2]{0,1:T(2,128)}, u32[]{:S(2)}) copy-start(s32[8,2]{0,1:T(2,128)} %param.4) | copy-start | bytes 196
  467.6 349.5 %reduce-scatter.2.cloned.1.call-start = ((), (), s32[]{:S(2)}) async-start(), calls=%async_computation.2 | async-start | bytes 3145728 | tf_op jit(solution)/shard_map/reduce_scatter | solution.py:32
  750.1 67.0 %copy-start = (f32[2,256,512]{2,1,0:T(8,128)S(1)}, f32[2,256,512]{2,1,0:T(8,128)}, u32[]{:S(2)}) copy-start(f32[2,256,512]{2,1,0:T(8,128)} %param.5) | copy-start | bytes 3145732
Sparse Core Ops, SparseCore 0:
  467.7 272.6 all-gather.1
  752.3 64.7 reduce-scatter.1
where the time goes:
time: 827 us; the launch traced here: 826 us
  blocking collectives  459 us (56%)
  waiting for transfers between devices  337 us (41%)
  between operations  13.5 us (2%)
  local copies, waits for them, and re-layouts  10 us (1%)
    psum x1, blocking collectives, body(): lax.psum(local_block.astype(jnp.float32), 'rep').astype(jnp.bfloat16)  459 us
    all_gather x1, waiting for transfers between devices, body(): whole_rows = lax.all_gather(summed_block, 'fsdp', axis=0, tiled=True)  272 us
    reduce_scatter x1, waiting for transfers between devices, body(): lax.psum_scatter(partial_tiles, 'tp', scatter_dimension=1, tiled=True)  64.9 us
  transfers between devices with their start and end apart: 2, of which 2 were waited for; matrix products, arithmetic and copies ran while one was open for 0% of the time, Pallas kernels for 0%

commit v1 on v0

v1 whole, which is shorter than its diff:
```python
import jax
import jax.numpy as jnp
from jax import lax
from jax.experimental import pallas as pl
from jax.experimental.pallas import tpu as pltpu
from jax.sharding import Mesh
from jax.sharding import PartitionSpec as P

Y, ZL, X, F, T = 8, 3, 4, 4, 2
NEAR = ZL * X
REP = Y * NEAR
TILE = 512
HERE = 8
PANELS = HERE * F
PICKS = 4
LANES = 128
SUB = 8
QUARTERS = TILE // LANES


def pick_kernel(index_ref, table_ref, out_ref):
    def step(n, carry):
        for k in range(PICKS):
            out_ref[n, k] = table_ref[index_ref[n * PICKS + k]]
        return carry

    lax.fori_loop(0, REP, step, 0)


def pick_pieces(index, table):
    return pl.pallas_call(
        pick_kernel,
        out_shape=jax.ShapeDtypeStruct((REP, PICKS, SUB, LANES), table.dtype),
        in_specs=[
            pl.BlockSpec(memory_space=pltpu.SMEM),
            pl.BlockSpec(memory_space=pltpu.VMEM),
        ],
        out_specs=pl.BlockSpec(memory_space=pltpu.VMEM),
        compiler_params=pltpu.CompilerParams(vmem_limit_bytes=16 * 2**20),
        cost_estimate=pl.CostEstimate(flops=0, bytes_accessed=2 * 2**20, transcendentals=0),
    )(index, table)


def body(grads, slot_panels, factor_old):
    width = grads.shape[2]
    rows = grads.shape[1]
    place = lax.axis_index("fsdp")
    own = lax.dynamic_index_in_dim(slot_panels.reshape(F, PICKS), place, 0, keepdims=False)
    columns = grads[0].T.reshape(NEAR, width // NEAR, rows)
    note = jnp.pad(own.astype(grads.dtype), (0, LANES - PICKS))
    note = jnp.broadcast_to(note, (NEAR, width // NEAR, LANES))
    with jax.named_scope("exchange_near"):
        came = lax.all_to_all(
            jnp.concatenate([columns, note], axis=2), ("zl", "x"), 0, 0, tiled=True
        )
    near_sum = came[:, :, :rows].astype(jnp.float32).sum(0)
    near_ends = came[:, 0, rows : rows + PICKS].astype(jnp.float32)

    blocks = near_sum.reshape(2, SUB, HERE, QUARTERS, LANES).transpose(0, 3, 2, 1, 4)
    blocks = blocks.reshape(Y, HERE * SUB, LANES)
    note = jnp.pad(near_ends.reshape(-1), (0, SUB * LANES - NEAR * PICKS)).reshape(SUB, LANES)
    note = jnp.broadcast_to(note, (Y, SUB, LANES))
    with jax.named_scope("exchange_y"):
        came = lax.all_to_all(
            jnp.concatenate([blocks, note], axis=1), "y", 0, 0, tiled=True
        )
    summed = came[:, : HERE * SUB].sum(0).astype(jnp.bfloat16)
    ends = came[:, HERE * SUB, : NEAR * PICKS].reshape(REP * PICKS).astype(jnp.int32)

    with jax.named_scope("gather_fsdp"):
        table = lax.all_to_all(
            jnp.broadcast_to(summed, (F, HERE * SUB, LANES)), "fsdp", 0, 0, tiled=True
        )
    table = table.reshape(PANELS, SUB, LANES)
    with jax.named_scope("pick"):
        pieces = pick_pieces(jnp.maximum(ends, 0), table)
    with jax.named_scope("exchange_panels"):
        came = lax.all_to_all(
            pieces.reshape(REP, PICKS * SUB, LANES), ("y", "zl", "x"), 0, 0, tiled=True
        )
    came = came.reshape(2, QUARTERS, NEAR, 2, 2, SUB, LANES)
    panels = came.transpose(3, 4, 2, 0, 5, 1, 6).reshape(2, 2, width, TILE)
    first = panels[:, 0].reshape(2, width, T, TILE // T).transpose(2, 0, 1, 3)
    second = jnp.broadcast_to(panels[:, 1], (T, 2, width, TILE))
    with jax.named_scope("exchange_tp"):
        both = lax.all_to_all(
            jnp.concatenate([first, second], axis=3), "tp", 0, 0, tiled=True
        )
    first = both[..., : TILE // T]
    second = both[..., TILE // T :]
    product = jnp.einsum("tsca,tscb->sab", first, second, preferred_element_type=jnp.float32)
    valid = own[0::2] >= 0
    product = jnp.where(valid[:, None, None], product, 0.0)
    return 0.9 * factor_old + 0.1 * product


def solution(mesh):
    fine = Mesh(mesh.devices.reshape(Y, ZL, X, F, T), ("y", "zl", "x", "fsdp", "tp"))
    rep = ("y", "zl", "x")
    placed = (P(rep, "fsdp", "tp"), P(rep, None), P(rep + ("fsdp",), "tp", None))
    return jax.shard_map(
        body, mesh=fine, in_specs=placed, out_specs=P(rep + ("fsdp",), "tp", None), check_vma=False
    )
```

time: 827 us -> 121 us (0.15)
  blocking collectives: 459 us -> 59.5 us
  waiting for transfers between devices: 337 us -> 30.8 us
  starting transfers between devices: 0.04 us -> 21.4 us
  between operations: 13.5 us -> 0.12 us
    psum x1 -> x0, blocking collectives: 459 us -> none  [body(): lax.psum(local_block.astype(jnp.float32), 'rep').astype(jnp.bfloat16)]
    all_gather x1 -> x0, waiting for transfers between devices: 272 us -> none  [body(): whole_rows = lax.all_gather(summed_block, 'fsdp', axis=0, tiled=True)]
    reduce_scatter x1 -> x0, waiting for transfers between devices: 64.9 us -> none  [body(): lax.psum_scatter(partial_tiles, 'tp', scatter_dimension=1, tiled=True)]
    all_to_all x0 -> x3, blocking collectives: none -> 59.5 us  [the longest x1 32 us: body(): lax.all_to_all(jnp.concatenate([columns, note], axis=2), ('zl', 'x'), 0,...]
    all_to_all x0 -> x2, waiting for transfers between devices: none -> 30.8 us  [the longest x1 21.5 us: body(): lax.all_to_all(pieces.reshape(REP, PICKS * SUB, LANES), ('y', 'zl', 'x'),...]
    all_to_all x0 -> x2, starting transfers between devices: none -> 21.4 us  [the longest x1 14.2 us: body(): lax.all_to_all(jnp.broadcast_to(summed, (F, HERE * SUB, LANES)), 'fsdp',...]
where the time goes in v1:
time: 121 us; the launch traced here: 120 us
  blocking collectives  59.5 us (49%)
  waiting for transfers between devices  30.8 us (25%)
  starting transfers between devices  21.4 us (18%)
  local copies, waits for them, and re-layouts  2.58 us (2%)
  Pallas kernels  2.39 us (2%)
  other arithmetic  2.06 us (2%)
  matrix products  1.49 us (1%)
    all_to_all x1, blocking collectives, body(): lax.all_to_all(jnp.concatenate([columns, note], axis=2), ('zl', 'x'), 0,...  32 us
    all_to_all x1, waiting for transfers between devices, body(): lax.all_to_all(pieces.reshape(REP, PICKS * SUB, LANES), ('y', 'zl', 'x'),...  21.5 us
    all_to_all x1, blocking collectives, body(): lax.all_to_all(jnp.concatenate([blocks, note], axis=1), 'y', 0, 0, tiled=...  19.9 us
    all_to_all x1, starting transfers between devices, body(): lax.all_to_all(jnp.broadcast_to(summed, (F, HERE * SUB, LANES)), 'fsdp',...  14.2 us
    all_to_all x1, waiting for transfers between devices, body(): lax.all_to_all(jnp.broadcast_to(summed, (F, HERE * SUB, LANES)), 'fsdp',...  9.28 us
    all_to_all x1, blocking collectives, body(): lax.all_to_all(jnp.concatenate([first, second], axis=3), 'tp', 0, 0, tile...  7.59 us
    all_to_all x1, starting transfers between devices, body(): lax.all_to_all(pieces.reshape(REP, PICKS * SUB, LANES), ('y', 'zl', 'x'),...  7.18 us
  transfers between devices with their start and end apart: 2, of which 2 were waited for; matrix products, arithmetic and copies ran while one was open for 0% of the time, Pallas kernels for 0%

profile of v1, /device:TPU:1, one launch (start us, length us, event | category | flops | bytes accessed | tf_op | source)
XLA Modules:
  0.0 120.3 jit_solution(11514615875274655029)
XLA Ops:
  0.0 0.8 copy.16
  0.8 0.1 reshape.38
  0.9 1.7 %pad_maximum_fusion = bf16[12,16,4224]{2,1,0:T(8,128)(2,1)S(1)} fusion(bf16[12,16,4096]{2,1,0:T(8,128)(2,1)} %bitcast.39, bf16[4224]{0:T(1024)(128)(2,1)S(1)} %fusion.5), kind=kLoop, calls=%fused_computation.1 | loop fusion | flops 3244032 | bytes 3203328 | tf_op jit(solution)/shard_map/exchange_near/concatenate | solution.py:54
  2.5 32.0 %all_to_all.25 = bf16[12,16,4224]{2,1,0:T(8,128)(2,1)S(1)} all-to-all(bf16[12,16,4224]{2,1,0:T(8,128)(2,1)S(1)} %pad_maximum_fusion), channel_id=1, replica_groups=mesh['y'=8,'zl'=3,'x'=4,'fsdp'=4,'tp'=2] {'zl','x'}, dimensions={0} | all-to-all | bytes 3244032 | tf_op jit(solution)/shard_map/exchange_near/all_to_all | solution.py:53
  34.6 0.1 convert_element_type.24
  34.6 0.2 convert_reduce_fusion
  34.9 0.2 reshape.40
  35.1 0.2 copy.17
  35.3 19.9 %all_to_all.26 = f32[8,72,128]{2,1,0:T(8,128)S(1)} all-to-all(f32[8,72,128]{2,1,0:T(8,128)S(1)} %pad_maximum_fusion.2), channel_id=1, replica_groups=mesh['y'=8,'zl'=3,'x'=4,'fsdp'=4,'tp'=2] {'y'}, dimensions={0} | all-to-all | bytes 589824 | tf_op jit(solution)/shard_map/exchange_y/all_to_all | solution.py:64
  55.2 0.6 broadcast_in_dim.28
  55.9 14.2 %all-to-all-start.2 = ((bf16[4,64,128]{2,1,0:T(8,128)(2,1)}), bf16[4,64,128]{2,1,0:T(8,128)(2,1)S(1)}, u32[]{:S(2)}, u32[]{:S(2)}) async-start(bf16[4,64,128]{2,1,0:T(8,128)(2,1)} %broadcast_in_dim.28), calls=%async_computation.2 | async-start | bytes 131072 | tf_op jit(solution)/shard_map/gather_fsdp/all_to_all | solution.py:71
  70.1 0.1 max.10.index_ref
  70.2 9.3 %all-to-all-done.2 = bf16[4,64,128]{2,1,0:T(8,128)(2,1)S(1)} async-done(((bf16[4,64,128]{2,1,0:T(8,128)(2,1)}), bf16[4,64,128]{2,1,0:T(8,128)(2,1)S(1)}, u32[]{:S(2)}, u32[]{:S(2)}) %all-to-all-start.2) | async-done | bytes 65568 | tf_op jit(solution)/shard_map/gather_fsdp/all_to_all | solution.py:71
  79.5 2.4 %pick.1 = bf16[96,4,8,128]{3,2,1,0:T(8,128)(2,1)} custom-call(s32[384]{0:T(512)S(1)} %max.10.index_ref, bf16[32,8,128]{2,1,0:T(8,128)(2,1)S(1)} %bitcast.35), custom_call_target="tpu_custom_call" | custom-call | bytes 2097152 | tf_op jit(solution)/shard_map/pick/pallas_call | solution.py:31
  81.9 7.2 %all-to-all-start.3 = ((bf16[96,32,128]{2,1,0:T(8,128)(2,1)}), bf16[96,32,128]{2,1,0:T(8,128)(2,1)S(1)}, u32[]{:S(2)}, u32[]{:S(2)}) async-start(bf16[96,32,128]{2,1,0:T(8,128)(2,1)} %bitcast.8), calls=%async_computation.3 | async-start | bytes 1572864 | tf_op jit(solution)/shard_map/exchange_panels/all_to_all | solution.py:78
  89.1 0.1 slice.27
  89.2 21.5 %all-to-all-done.3 = bf16[96,32,128]{2,1,0:T(8,128)(2,1)S(1)} async-done(((bf16[96,32,128]{2,1,0:T(8,128)(2,1)}), bf16[96,32,128]{2,1,0:T(8,128)(2,1)S(1)}, u32[]{:S(2)}, u32[]{:S(2)}) %all-to-all-start.3) | async-done | bytes 786464 | tf_op jit(solution)/shard_map/exchange_panels/all_to_all | solution.py:78
  110.7 0.2 copy.18
  110.9 0.1 fusion.9
  111.0 0.1 reshape_squeeze.4
  111.1 0.1 broadcast_in_dim.29
  111.2 0.1 pad_maximum_fusion.1
  111.3 0.0 copy-start
  111.3 7.6 %all_to_all.27 = bf16[2,2,192,768]{3,2,1,0:T(8,128)(2,1)S(1)} all-to-all(bf16[2,2,192,768]{3,2,1,0:T(8,128)(2,1)S(1)} %pad_maximum_fusion.1), channel_id=1, replica_groups=mesh['y'=8,'zl'=3,'x'=4,'fsdp'=4,'tp'=2] {'tp'}, dimensions={0} | all-to-all | bytes 2359296 | tf_op jit(solution)/shard_map/exchange_tp/all_to_all | solution.py:86
  118.9 0.0 copy-done
  118.9 1.5 %fusion.2 = f32[2,256,512]{2,1,0:T(8,128)} fusion(f32[2,256,512]{2,1,0:T(8,128)S(1)} %copy-done, pred[2]{0:T(512)(128)(4,1)S(1)} %broadcast_compare_fusion, bf16[2,2,192,768]{3,2,1,0:T(8,128)(2,1)S(1)} %all_to_all.27), kind=kOutput, calls=%fused_computation.5 | convolution fusion | flops 202375168 | bytes 3276802 | tf_op jit(solution)/shard_map/tsca,tscb->sab/dot_general | solution.py:91
  (10 shorter events, 0.2 us)
Async XLA Ops:
  55.9 23.6 %all-to-all-start.2 = ((bf16[4,64,128]{2,1,0:T(8,128)(2,1)}), bf16[4,64,128]{2,1,0:T(8,128)(2,1)S(1)}, u32[]{:S(2)}, u32[]{:S(2)}) async-start(bf16[4,64,128]{2,1,0:T(8,128)(2,1)} %broadcast_in_dim.28), calls=%async_computation.2 | async-start | bytes 131072 | tf_op jit(solution)/shard_map/gather_fsdp/all_to_all | solution.py:71
  81.9 28.8 %all-to-all-start.3 = ((bf16[96,32,128]{2,1,0:T(8,128)(2,1)}), bf16[96,32,128]{2,1,0:T(8,128)(2,1)S(1)}, u32[]{:S(2)}, u32[]{:S(2)}) async-start(bf16[96,32,128]{2,1,0:T(8,128)(2,1)} %bitcast.8), calls=%async_computation.3 | async-start | bytes 1572864 | tf_op jit(solution)/shard_map/exchange_panels/all_to_all | solution.py:78
  111.3 7.6 %copy-start = (f32[2,256,512]{2,1,0:T(8,128)S(1)}, f32[2,256,512]{2,1,0:T(8,128)}, u32[]{:S(2)}) copy-start(f32[2,256,512]{2,1,0:T(8,128)} %param.5) | copy-start | bytes 3145732

commit v2 on v1

v2 whole, which is shorter than its diff:
```python
import jax
import jax.numpy as jnp
from jax import lax
from jax.experimental import pallas as pl
from jax.experimental.pallas import tpu as pltpu
from jax.sharding import Mesh
from jax.sharding import PartitionSpec as P

YH, YL, ZL, X, F, T = 4, 2, 3, 4, 4, 2
NEAR = YL * ZL * X
PLANE = YH * YL * X
TILE = 512
HERE = 8
PANELS = HERE * F
PICKS = 4
LANES = 128
SUB = 8


def pick_kernel(index_ref, table_ref, out_ref):
    def step(n, carry):
        for k in range(PICKS):
            panel = index_ref[n * PICKS + k]
            for z in range(ZL):
                out_ref[n, k, z] = table_ref[z * PANELS + panel]
        return carry

    lax.fori_loop(0, PLANE, step, 0, unroll=4)


def pick_pieces(index, table):
    return pl.pallas_call(
        pick_kernel,
        out_shape=jax.ShapeDtypeStruct((PLANE, PICKS, ZL, SUB, LANES), table.dtype),
        in_specs=[
            pl.BlockSpec(memory_space=pltpu.SMEM),
            pl.BlockSpec(memory_space=pltpu.VMEM),
        ],
        out_specs=pl.BlockSpec(memory_space=pltpu.VMEM),
        compiler_params=pltpu.CompilerParams(vmem_limit_bytes=16 * 2**20),
        cost_estimate=pl.CostEstimate(flops=0, bytes_accessed=2 * 2**20, transcendentals=0),
    )(index, table)


def body(grads, slot_panels, factor_old):
    width = grads.shape[2]
    rows = grads.shape[1]
    place = lax.axis_index("fsdp")
    turn = jnp.arange(F * 2, dtype=jnp.int32)[:, None]
    own = [jnp.where(turn == 2 * place + s, slot_panels, 0).sum(0) for s in range(2)]
    own = jnp.concatenate(own)
    columns = grads[0].T.reshape(NEAR, SUB, rows)
    note = jnp.pad(own.astype(grads.dtype), (0, LANES - PICKS))
    note = jnp.broadcast_to(note, (NEAR, SUB, LANES))
    with jax.named_scope("exchange_near"):
        came = lax.all_to_all(
            jnp.concatenate([columns, note], axis=2), ("yl", "zl", "x"), 0, 0, tiled=True
        )
    near_sum = came[:, :, :rows].astype(jnp.float32).sum(0)
    near_ends = came[:, 0, rows : rows + PICKS].astype(jnp.float32)

    blocks = near_sum.reshape(SUB, HERE, YH, LANES).transpose(2, 1, 0, 3)
    blocks = blocks.reshape(YH, HERE * SUB, LANES)
    note = jnp.pad(near_ends.reshape(-1), (0, LANES - NEAR * PICKS))
    note = jnp.broadcast_to(note, (YH, SUB, LANES))
    with jax.named_scope("exchange_far"):
        came = lax.all_to_all(
            jnp.concatenate([blocks, note], axis=1), "yh", 0, 0, tiled=True
        )
    summed = came[:, : HERE * SUB].sum(0).astype(jnp.bfloat16)
    ends = came[:, HERE * SUB, : NEAR * PICKS].astype(jnp.int32)
    ends = ends.reshape(YH, YL, ZL, X * PICKS)
    ends = lax.dynamic_index_in_dim(ends, lax.axis_index("zl"), 2, keepdims=False)
    ends = jnp.maximum(ends, 0).reshape(PLANE * PICKS)

    with jax.named_scope("gather_z"):
        table = lax.all_to_all(
            jnp.broadcast_to(summed, (ZL * F, HERE * SUB, LANES)), ("zl", "fsdp"), 0, 0, tiled=True
        )
    table = table.reshape(ZL * PANELS, SUB, LANES)
    with jax.named_scope("pick"):
        pieces = pick_pieces(ends, table)
    with jax.named_scope("exchange_panels"):
        came = lax.all_to_all(
            pieces.reshape(PLANE, PICKS * ZL * SUB, LANES), ("yh", "yl", "x"), 0, 0, tiled=True
        )
    came = came.reshape(YH, YL, X, 2, 2, ZL, SUB, LANES)
    panels = came.transpose(3, 4, 1, 5, 2, 6, 0, 7).reshape(2, 2, width, TILE)
    first = panels[:, 0].reshape(2, width, T, TILE // T).transpose(2, 0, 1, 3)
    second = jnp.broadcast_to(panels[:, 1], (T, 2, width, TILE))
    with jax.named_scope("exchange_tp"):
        both = lax.all_to_all(
            jnp.concatenate([first, second], axis=3), "tp", 0, 0, tiled=True
        )
    first = both[..., : TILE // T]
    second = both[..., TILE // T :]
    product = jnp.einsum("tsca,tscb->sab", first, second, preferred_element_type=jnp.float32)
    valid = own[0::2] >= 0
    product = jnp.where(valid[:, None, None], product, 0.0)
    return 0.9 * factor_old + 0.1 * product


def solution(mesh):
    fine = Mesh(
        mesh.devices.reshape(YH, YL, ZL, X, F, T), ("yh", "yl", "zl", "x", "fsdp", "tp")
    )
    rep = ("yh", "yl", "zl", "x")
    placed = (P(rep, "fsdp", "tp"), P(rep, None), P(rep + ("fsdp",), "tp", None))
    return jax.shard_map(
        body, mesh=fine, in_specs=placed, out_specs=P(rep + ("fsdp",), "tp", None), check_vma=False
    )
```

time: 121 us -> 116 us (0.959)
  starting transfers between devices: 21.4 us -> 18.1 us
  waiting for transfers between devices: 30.8 us -> 27.6 us
  blocking collectives: 59.5 us -> 62.1 us
    all_to_all x1, blocking collectives: 7.59 us -> 11.5 us  [body(): lax.all_to_all(jnp.concatenate([first, second], axis=3), 'tp', 0, 0, tile...]
    all_to_all x2, starting transfers between devices: 21.4 us -> 18.1 us  [the longest x1 14.2 us: body(): lax.all_to_all(jnp.broadcast_to(summed, (ZL * F, HERE * SUB, LANES)), ('z...]
    all_to_all x2, waiting for transfers between devices: 30.8 us -> 27.6 us  [the longest x1 16.7 us: body(): lax.all_to_all(pieces.reshape(PLANE, PICKS * ZL * SUB, LANES), ('yh', 'yl...]
    all_to_all x2, blocking collectives: 51.9 us -> 50.6 us  [the longest x1 34.5 us: body(): lax.all_to_all(jnp.concatenate([columns, note], axis=2), ('yl', 'zl', 'x'...]
where the time goes in v2:
time: 116 us
  blocking collectives  62.1 us (54%)
  waiting for transfers between devices  27.6 us (24%)
  starting transfers between devices  18.1 us (16%)
  other arithmetic  2.98 us (3%)
  local copies, waits for them, and re-layouts  1.79 us (2%)
  Pallas kernels  1.67 us (1%)
  matrix products  1.48 us (1%)
    all_to_all x1, blocking collectives, body(): lax.all_to_all(jnp.concatenate([columns, note], axis=2), ('yl', 'zl', 'x'...  34.5 us
    all_to_all x1, waiting for transfers between devices, body(): lax.all_to_all(pieces.reshape(PLANE, PICKS * ZL * SUB, LANES), ('yh', 'yl...  16.7 us
    all_to_all x1, blocking collectives, body(): lax.all_to_all(jnp.concatenate([blocks, note], axis=1), 'yh', 0, 0, tiled...  16.2 us
    all_to_all x1, starting transfers between devices, body(): lax.all_to_all(jnp.broadcast_to(summed, (ZL * F, HERE * SUB, LANES)), ('z...  14.2 us
    all_to_all x1, blocking collectives, body(): lax.all_to_all(jnp.concatenate([first, second], axis=3), 'tp', 0, 0, tile...  11.5 us
    all_to_all x1, waiting for transfers between devices, body(): lax.all_to_all(jnp.broadcast_to(summed, (ZL * F, HERE * SUB, LANES)), ('z...  10.8 us
    all_to_all x1, starting transfers between devices, body(): lax.all_to_all(pieces.reshape(PLANE, PICKS * ZL * SUB, LANES), ('yh', 'yl...  3.91 us
  transfers between devices with their start and end apart: 2, of which 2 were waited for; matrix products, arithmetic and copies ran while one was open for 0% of the time, Pallas kernels for 0%

profile of v2, /device:TPU:1, one launch (start us, length us, event | category | flops | bytes accessed | tf_op | source)
XLA Modules:
  0.0 115.9 jit_solution(13537965402435481489)
XLA Ops:
  0.0 0.8 select_reduce_fusion.1
  0.8 0.1 fusion.7
  0.9 1.7 %pad_maximum_fusion = bf16[24,8,4224]{2,1,0:T(8,128)(2,1)S(1)} fusion(bf16[24,8,4096]{2,1,0:T(8,128)(2,1)} %bitcast.35, bf16[4224]{0:T(1024)(128)(2,1)S(1)} %fusion.5), kind=kLoop, calls=%fused_computation.1 | loop fusion | flops 3244032 | bytes 3203328 | tf_op jit(solution)/shard_map/exchange_near/concatenate | solution.py:57
  2.6 34.5 %all_to_all.25 = bf16[24,8,4224]{2,1,0:T(8,128)(2,1)S(1)} all-to-all(bf16[24,8,4224]{2,1,0:T(8,128)(2,1)S(1)} %pad_maximum_fusion), channel_id=1, replica_groups=mesh['yh'=4,'yl'=2,'zl'=3,'x'=4,'fsdp'=4,'tp'=2] {'yl','zl','x'}, dimensions={0} | all-to-all | bytes 3244032 | tf_op jit(solution)/shard_map/exchange_near/all_to_all | solution.py:56
  37.1 0.1 convert_element_type.27
  37.2 0.2 convert_reduce_fusion
  37.4 0.1 reshape.44
  37.6 0.1 copy.26
  37.7 16.2 %all_to_all.26 = f32[4,72,128]{2,1,0:T(8,128)S(1)} all-to-all(f32[4,72,128]{2,1,0:T(8,128)S(1)} %pad_maximum_fusion.2), channel_id=1, replica_groups=mesh['yh'=4,'yl'=2,'zl'=3,'x'=4,'fsdp'=4,'tp'=2] {'yh'}, dimensions={0} | all-to-all | bytes 294912 | tf_op jit(solution)/shard_map/exchange_far/all_to_all | solution.py:67
  53.9 0.7 broadcast_in_dim.50
  54.6 14.2 %all-to-all-start.2 = ((bf16[12,64,128]{2,1,0:T(8,128)(2,1)}), bf16[12,64,128]{2,1,0:T(8,128)(2,1)S(1)}, u32[]{:S(2)}, u32[]{:S(2)}) async-start(bf16[12,64,128]{2,1,0:T(8,128)(2,1)} %broadcast_in_dim.50), calls=%async_computation.2 | async-start | bytes 393216 | tf_op jit(solution)/shard_map/gather_z/all_to_all | solution.py:77
  68.8 0.1 convert_element_type.29
  69.0 0.1 max.12.index_ref
  69.0 10.8 %all-to-all-done.2 = bf16[12,64,128]{2,1,0:T(8,128)(2,1)S(1)} async-done(((bf16[12,64,128]{2,1,0:T(8,128)(2,1)}), bf16[12,64,128]{2,1,0:T(8,128)(2,1)S(1)}, u32[]{:S(2)}, u32[]{:S(2)}) %all-to-all-start.2) | async-done | bytes 196640 | tf_op jit(solution)/shard_map/gather_z/all_to_all | solution.py:77
  79.9 1.7 %pick.1 = bf16[32,4,3,8,128]{4,3,2,1,0:T(8,128)(2,1)} custom-call(s32[128]{0:T(128)S(1)} %max.12.index_ref, bf16[96,8,128]{2,1,0:T(8,128)(2,1)S(1)} %bitcast.31), custom_call_target="tpu_custom_call" | custom-call | bytes 2097152 | tf_op jit(solution)/shard_map/pick/pallas_call | solution.py:32
  81.5 3.9 %all-to-all-start.3 = ((bf16[32,96,128]{2,1,0:T(8,128)(2,1)}), bf16[32,96,128]{2,1,0:T(8,128)(2,1)S(1)}, u32[]{:S(2)}, u32[]{:S(2)}) async-start(bf16[32,96,128]{2,1,0:T(8,128)(2,1)} %bitcast.6), calls=%async_computation.3 | async-start | bytes 1572864 | tf_op jit(solution)/shard_map/exchange_panels/all_to_all | solution.py:84
  85.5 0.1 slice.27
  85.6 16.7 %all-to-all-done.3 = bf16[32,96,128]{2,1,0:T(8,128)(2,1)S(1)} async-done(((bf16[32,96,128]{2,1,0:T(8,128)(2,1)}), bf16[32,96,128]{2,1,0:T(8,128)(2,1)S(1)}, u32[]{:S(2)}, u32[]{:S(2)}) %all-to-all-start.3) | async-done | bytes 786464 | tf_op jit(solution)/shard_map/exchange_panels/all_to_all | solution.py:84
  102.3 0.2 copy.14
  102.5 0.1 fusion.8
  102.6 0.1 reshape_squeeze.3
  102.7 0.1 broadcast_in_dim.51
  102.8 0.1 pad_maximum_fusion.1
  102.9 0.0 copy-start
  102.9 11.5 %all_to_all.27 = bf16[2,2,192,768]{3,2,1,0:T(8,128)(2,1)S(1)} all-to-all(bf16[2,2,192,768]{3,2,1,0:T(8,128)(2,1)S(1)} %pad_maximum_fusion.1), channel_id=1, replica_groups=mesh['yh'=4,'yl'=2,'zl'=3,'x'=4,'fsdp'=4,'tp'=2] {'tp'}, dimensions={0} | all-to-all | bytes 2359296 | tf_op jit(solution)/shard_map/exchange_tp/all_to_all | solution.py:92
  114.4 0.0 copy-done
  114.4 1.5 %fusion.2 = f32[2,256,512]{2,1,0:T(8,128)} fusion(f32[2,256,512]{2,1,0:T(8,128)S(1)} %copy-done, pred[2]{0:T(512)(128)(4,1)S(1)} %broadcast_compare_fusion, bf16[2,2,192,768]{3,2,1,0:T(8,128)(2,1)S(1)} %all_to_all.27), kind=kOutput, calls=%fused_computation.5 | convolution fusion | flops 202375168 | bytes 3276802 | tf_op jit(solution)/shard_map/tsca,tscb->sab/dot_general | solution.py:97
  (11 shorter events, 0.2 us)
Async XLA Ops:
  54.6 25.3 %all-to-all-start.2 = ((bf16[12,64,128]{2,1,0:T(8,128)(2,1)}), bf16[12,64,128]{2,1,0:T(8,128)(2,1)S(1)}, u32[]{:S(2)}, u32[]{:S(2)}) async-start(bf16[12,64,128]{2,1,0:T(8,128)(2,1)} %broadcast_in_dim.50), calls=%async_computation.2 | async-start | bytes 393216 | tf_op jit(solution)/shard_map/gather_z/all_to_all | solution.py:77
  81.5 20.8 %all-to-all-start.3 = ((bf16[32,96,128]{2,1,0:T(8,128)(2,1)}), bf16[32,96,128]{2,1,0:T(8,128)(2,1)S(1)}, u32[]{:S(2)}, u32[]{:S(2)}) async-start(bf16[32,96,128]{2,1,0:T(8,128)(2,1)} %bitcast.6), calls=%async_computation.3 | async-start | bytes 1572864 | tf_op jit(solution)/shard_map/exchange_panels/all_to_all | solution.py:84
  102.9 11.5 %copy-start = (f32[2,256,512]{2,1,0:T(8,128)S(1)}, f32[2,256,512]{2,1,0:T(8,128)}, u32[]{:S(2)}) copy-start(f32[2,256,512]{2,1,0:T(8,128)} %param.5) | copy-start | bytes 3145732

commit v3 on v2

--- a/solution.py
+++ b/solution.py
@@ -15,14 +15,62 @@
 PICKS = 4
 LANES = 128
 SUB = 8
+CHUNKS = 6
+
+
+def note_kernel(ends_ref, columns_ref, out_ref, note_ref, sems):
+    width, rows = columns_ref.shape
+    step = width // CHUNKS
+    copies = []
+    for n in range(CHUNKS):
+        part = pl.ds(n * step, step)
+        copies.append(
+            pltpu.make_async_copy(
+                columns_ref.at[part], out_ref.at[part, pl.ds(0, rows)], sems.at[n]
+            )
+        )
+        copies[-1].start()
+    place = lax.axis_index("fsdp")
+    lane = lax.broadcasted_iota(jnp.int32, note_ref.shape, 1)
+    note = jnp.zeros(note_ref.shape, jnp.int32)
+    for slot in range(2):
+        for end in range(2):
+            note = jnp.where(lane == 2 * slot + end, ends_ref[end, 2 * place + slot], note)
+    note_ref[...] = note.astype(jnp.float32).astype(note_ref.dtype)
+    copies.append(
+        pltpu.make_async_copy(note_ref, out_ref.at[:, pl.ds(rows, LANES)], sems.at[CHUNKS])
+    )
+    copies[-1].start()
+    for copy in copies:
+        copy.wait()
+
+
+def add_note(slot_panels, columns):
+    width, rows = columns.shape
+    return pl.pallas_call(
+        note_kernel,
+        out_shape=jax.ShapeDtypeStruct((width, rows + LANES), columns.dtype),
+        in_specs=[
+            pl.BlockSpec(memory_space=pltpu.SMEM),
+            pl.BlockSpec(memory_space=pl.ANY),
+        ],
+        out_specs=pl.BlockSpec(memory_space=pl.ANY),
+        scratch_shapes=[
+            pltpu.VMEM((width, LANES), columns.dtype),
+            pltpu.SemaphoreType.DMA((CHUNKS + 1,)),
+        ],
+        compiler_params=pltpu.CompilerParams(vmem_limit_bytes=16 * 2**20),
+        cost_estimate=pl.CostEstimate(flops=0, bytes_accessed=3 * 2**20, transcendentals=0),
+    )(slot_panels.T, columns)
 
 
 def pick_kernel(index_ref, table_ref, out_ref):
     def step(n, carry):
+        panels = [index_ref[n * PICKS + k] for k in range(PICKS)]
+        found = [[table_ref[z * PANELS + panel] for z in range(ZL)] for panel in panels]
         for k in range(PICKS):
-            panel = index_ref[n * PICKS + k]
             for z in range(ZL):
-                out_ref[n, k, z] = table_ref[z * PANELS + panel]
+                out_ref[n, k, z] = found[k][z]
         return carry
 
     lax.fori_loop(0, PLANE, step, 0, unroll=4)
@@ -49,12 +97,11 @@
     turn = jnp.arange(F * 2, dtype=jnp.int32)[:, None]
     own = [jnp.where(turn == 2 * place + s, slot_panels, 0).sum(0) for s in range(2)]
     own = jnp.concatenate(own)
-    columns = grads[0].T.reshape(NEAR, SUB, rows)
-    note = jnp.pad(own.astype(grads.dtype), (0, LANES - PICKS))
-    note = jnp.broadcast_to(note, (NEAR, SUB, LANES))
+    with jax.named_scope("add_note"):
+        noted = add_note(slot_panels, grads[0].T)
     with jax.named_scope("exchange_near"):
         came = lax.all_to_all(
-            jnp.concatenate([columns, note], axis=2), ("yl", "zl", "x"), 0, 0, tiled=True
+            noted.reshape(NEAR, SUB, rows + LANES), ("yl", "zl", "x"), 0, 0, tiled=True
         )
     near_sum = came[:, :, :rows].astype(jnp.float32).sum(0)
     near_ends = came[:, 0, rows : rows + PICKS].astype(jnp.float32)
@@ -84,17 +131,27 @@
         came = lax.all_to_all(
             pieces.reshape(PLANE, PICKS * ZL * SUB, LANES), ("yh", "yl", "x"), 0, 0, tiled=True
         )
-    came = came.reshape(YH, YL, X, 2, 2, ZL, SUB, LANES)
-    panels = came.transpose(3, 4, 1, 5, 2, 6, 0, 7).reshape(2, 2, width, TILE)
-    first = panels[:, 0].reshape(2, width, T, TILE // T).transpose(2, 0, 1, 3)
-    second = jnp.broadcast_to(panels[:, 1], (T, 2, width, TILE))
+    came = came.reshape(T, YH // T, YL, X, 2, 2, ZL, SUB, LANES)
+    second = came[..., 1, :, :, :].transpose(4, 2, 5, 3, 6, 0, 1, 7).reshape(2, width, TILE)
+    half = lax.axis_index("tp")
+
+    def row_half(place):
+        part = lax.dynamic_index_in_dim(came[..., 0, :, :, :], place, 0, keepdims=False)
+        return part.transpose(3, 1, 4, 2, 5, 0, 6).reshape(2, width, TILE // T)
+
     with jax.named_scope("exchange_tp"):
-        both = lax.all_to_all(
-            jnp.concatenate([first, second], axis=3), "tp", 0, 0, tiled=True
+        other = lax.ppermute(
+            jnp.concatenate([row_half(1 - half), second], axis=2), "tp", [(0, 1), (1, 0)]
         )
-    first = both[..., : TILE // T]
-    second = both[..., TILE // T :]
-    product = jnp.einsum("tsca,tscb->sab", first, second, preferred_element_type=jnp.float32)
+    product = jnp.einsum(
+        "sca,scb->sab", row_half(half), second, preferred_element_type=jnp.float32
+    )
+    product = product + jnp.einsum(
+        "sca,scb->sab",
+        other[..., : TILE // T],
+        other[..., TILE // T :],
+        preferred_element_type=jnp.float32,
+    )
     valid = own[0::2] >= 0
     product = jnp.where(valid[:, None, None], product, 0.0)
     return 0.9 * factor_old + 0.1 * product

time: 116 us -> 116 us (level)
  blocking collectives: 62.1 us -> 50.6 us
  starting transfers between devices: 18.1 us -> 27.2 us
  other arithmetic: 2.98 us -> 0.57 us
  local copies, waits for them, and re-layouts: 1.79 us -> 3.76 us
    all_to_all x2 -> x1, blocking collectives: 45.9 us -> 34.5 us  [body(): lax.all_to_all(noted.reshape(NEAR, SUB, rows + LANES), ('yl', 'zl', 'x'),...]
    ppermute x0 -> x1, starting transfers between devices: none -> 9.09 us  [body(): lax.ppermute(jnp.concatenate([row_half(1 - half), second], axis=2), 'tp',...]
    unnamed x2 -> x9, local copies, waits for them, and re-layouts: 0.01 us -> 2.19 us
    concatenate x3 -> x2, other arithmetic: 1.77 us -> 0.12 us  [the longest x1 0.08 us: body(): own = jnp.concatenate(own)]
  transfers between devices with their start and end apart: 2 -> 3, of which waited for: 2 -> 3; matrix products, arithmetic and copies ran while one was open for 0% -> 1% of each run, Pallas kernels for 0% -> 0%
where the time goes in v3:
time: 116 us; the launch traced here: 115 us
  blocking collectives  50.6 us (44%)
  waiting for transfers between devices  28.5 us (25%)
  starting transfers between devices  27.2 us (23%)
  local copies, waits for them, and re-layouts  3.76 us (3%)
  Pallas kernels  2.44 us (2%)
  matrix products  1.79 us (2%)
    all_to_all x1, blocking collectives, body(): lax.all_to_all(noted.reshape(NEAR, SUB, rows + LANES), ('yl', 'zl', 'x'),...  34.5 us
    all_to_all x1, waiting for transfers between devices, body(): lax.all_to_all(pieces.reshape(PLANE, PICKS * ZL * SUB, LANES), ('yh', 'yl...  16.7 us
    all_to_all x1, blocking collectives, body(): lax.all_to_all(jnp.concatenate([blocks, note], axis=1), 'yh', 0, 0, tiled...  16.2 us
    all_to_all x1, starting transfers between devices, body(): lax.all_to_all(jnp.broadcast_to(summed, (ZL * F, HERE * SUB, LANES)), ('z...  14.2 us
    all_to_all x1, waiting for transfers between devices, body(): lax.all_to_all(jnp.broadcast_to(summed, (ZL * F, HERE * SUB, LANES)), ('z...  10.8 us
    ppermute x1, starting transfers between devices, body(): lax.ppermute(jnp.concatenate([row_half(1 - half), second], axis=2), 'tp',...  9.09 us
    all_to_all x1, starting transfers between devices, body(): lax.all_to_all(pieces.reshape(PLANE, PICKS * ZL * SUB, LANES), ('yh', 'yl...  3.91 us
  transfers between devices with their start and end apart: 3, of which 3 were waited for; matrix products, arithmetic and copies ran while one was open for 1% of the time, Pallas kernels for 0%

profile of v3, /device:TPU:1, one launch (start us, length us, event | category | flops | bytes accessed | tf_op | source)
XLA Modules:
  0.0 115.1 jit_solution(4737162634305979581)
XLA Ops:
  0.0 0.0 copy-start
  0.0 1.4 %copy-done = bf16[1,4096,192]{1,2,0:T(8,128)(2,1)S(1)} copy-done((bf16[1,4096,192]{1,2,0:T(8,128)(2,1)S(1)}, bf16[1,4096,192]{1,2,0:T(8,128)(2,1)}, u32[]{:S(2)}) %copy-start) | copy-done | bytes 1572888
  1.4 0.0 copy-start.1
  1.4 0.7 copy-done.1
  2.1 0.8 add_note.1
  2.9 34.5 %all_to_all.20 = bf16[24,8,4224]{2,1,0:T(8,128)(2,1)S(1)} all-to-all(bf16[24,8,4224]{2,1,0:T(8,128)(2,1)S(1)} %bitcast.29), channel_id=1, replica_groups=mesh['yh'=4,'yl'=2,'zl'=3,'x'=4,'fsdp'=4,'tp'=2] {'yl','zl','x'}, dimensions={0} | all-to-all | bytes 3244032 | tf_op jit(solution)/shard_map/exchange_near/all_to_all | solution.py:103
  37.4 0.1 convert_element_type.21
  37.5 0.2 convert_reduce_fusion
  37.7 0.1 reshape.54
  37.8 0.1 copy.23
  37.9 16.2 %all_to_all.21 = f32[4,72,128]{2,1,0:T(8,128)S(1)} all-to-all(f32[4,72,128]{2,1,0:T(8,128)S(1)} %pad_maximum_fusion.1), channel_id=1, replica_groups=mesh['yh'=4,'yl'=2,'zl'=3,'x'=4,'fsdp'=4,'tp'=2] {'yh'}, dimensions={0} | all-to-all | bytes 294912 | tf_op jit(solution)/shard_map/exchange_far/all_to_all | solution.py:114
  54.1 0.0 copy-start.2
  54.1 0.7 broadcast_in_dim.43
  54.9 14.2 %all-to-all-start.2 = ((bf16[12,64,128]{2,1,0:T(8,128)(2,1)}), bf16[12,64,128]{2,1,0:T(8,128)(2,1)S(1)}, u32[]{:S(2)}, u32[]{:S(2)}) async-start(bf16[12,64,128]{2,1,0:T(8,128)(2,1)} %broadcast_in_dim.43), calls=%async_computation.2 | async-start | bytes 393216 | tf_op jit(solution)/shard_map/gather_z/all_to_all | solution.py:124
  69.1 0.1 convert_element_type.23
  69.2 0.1 max.12.index_ref
  69.3 10.8 %all-to-all-done.2 = bf16[12,64,128]{2,1,0:T(8,128)(2,1)S(1)} async-done(((bf16[12,64,128]{2,1,0:T(8,128)(2,1)}), bf16[12,64,128]{2,1,0:T(8,128)(2,1)S(1)}, u32[]{:S(2)}, u32[]{:S(2)}) %all-to-all-start.2) | async-done | bytes 196640 | tf_op jit(solution)/shard_map/gather_z/all_to_all | solution.py:124
  80.1 1.7 %pick.1 = bf16[32,4,3,8,128]{4,3,2,1,0:T(8,128)(2,1)} custom-call(s32[128]{0:T(128)S(1)} %max.12.index_ref, bf16[96,8,128]{2,1,0:T(8,128)(2,1)S(1)} %bitcast.31), custom_call_target="tpu_custom_call" | custom-call | bytes 2097152 | tf_op jit(solution)/shard_map/pick/pallas_call | solution.py:80
  81.8 3.9 %all-to-all-start.3 = ((bf16[32,96,128]{2,1,0:T(8,128)(2,1)}), bf16[32,96,128]{2,1,0:T(8,128)(2,1)S(1)}, u32[]{:S(2)}, u32[]{:S(2)}) async-start(bf16[32,96,128]{2,1,0:T(8,128)(2,1)} %bitcast.7), calls=%async_computation.3 | async-start | bytes 1572864 | tf_op jit(solution)/shard_map/exchange_panels/all_to_all | solution.py:131
  85.7 0.0 copy-done.2
  85.8 0.1 select_reduce_fusion.1
  85.9 16.7 %all-to-all-done.3 = bf16[32,96,128]{2,1,0:T(8,128)(2,1)S(1)} async-done(((bf16[32,96,128]{2,1,0:T(8,128)(2,1)}), bf16[32,96,128]{2,1,0:T(8,128)(2,1)S(1)}, u32[]{:S(2)}, u32[]{:S(2)}) %all-to-all-start.3) | async-done | bytes 786464 | tf_op jit(solution)/shard_map/exchange_panels/all_to_all | solution.py:131
  102.6 0.1 fusion.6
  102.7 0.1 copy.21
  102.8 0.1 constant_dynamic-slice_fusion
  102.9 0.0 copy-start.3
  103.0 9.1 %collective-permute-start = (bf16[2,192,768]{2,1,0:T(8,128)(2,1)S(1)}, bf16[2,192,768]{2,1,0:T(8,128)(2,1)S(1)}, u32[]{:S(2)}, u32[]{:S(2)}) collective-permute-start(bf16[2,192,768]{2,1,0:T(8,128)(2,1)S(1)} %pad_maximum_fusion), channel_id=1, source_target_pairs={{0,1},{1,0},{2,3},{3,2},{4,5},{5,4},{6,7},{7,6},{8,9},{9,8},{10,11... | collective-permute-start | bytes 1769480 | tf_op jit(solution)/shard_map/exchange_tp/ppermute | solution.py:143
  112.1 0.1 pad_add_fusion
  112.1 0.1 slice.28
  112.3 0.4 fusion.7
  112.6 1.0 collective-permute-done
  113.7 0.0 copy-done.3
  113.7 1.4 %fusion.2 = f32[2,256,512]{2,1,0:T(8,128)} fusion(f32[2,256,512]{2,1,0:T(8,128)S(1)} %fusion.7, f32[2,256,512]{2,1,0:T(8,128)S(1)} %copy-done.3, pred[2]{0:T(512)(128)(4,1)S(1)} %broadcast_compare_fusion, bf16[2,192,768]{2,1,0:T(8,128)(2,1)S(1)} %collective-permute-done), kind=kOutput, calls=%fused_computation.4 | convolution fusion | flops 101974016 | bytes 3735554 | tf_op jit(solution)/shard_map/sca,scb->sab/dot_general | solution.py:149
  (12 shorter events, 0.3 us)
Async XLA Ops:
  0.0 1.4 %copy-start = (bf16[1,4096,192]{1,2,0:T(8,128)(2,1)S(1)}, bf16[1,4096,192]{1,2,0:T(8,128)(2,1)}, u32[]{:S(2)}) copy-start(bf16[1,4096,192]{1,2,0:T(8,128)(2,1)} %param.3) | copy-start | bytes 4718596
  1.4 0.7 copy-start.1
  54.1 31.6 %copy-start.2 = (s32[8,2]{0,1:T(2,128)S(1)}, s32[8,2]{0,1:T(2,128)}, u32[]{:S(2)}) copy-start(s32[8,2]{0,1:T(2,128)} %param.4) | copy-start | bytes 196
  54.9 25.3 %all-to-all-start.2 = ((bf16[12,64,128]{2,1,0:T(8,128)(2,1)}), bf16[12,64,128]{2,1,0:T(8,128)(2,1)S(1)}, u32[]{:S(2)}, u32[]{:S(2)}) async-start(bf16[12,64,128]{2,1,0:T(8,128)(2,1)} %broadcast_in_dim.43), calls=%async_computation.2 | async-start | bytes 393216 | tf_op jit(solution)/shard_map/gather_z/all_to_all | solution.py:124
  81.8 20.8 %all-to-all-start.3 = ((bf16[32,96,128]{2,1,0:T(8,128)(2,1)}), bf16[32,96,128]{2,1,0:T(8,128)(2,1)S(1)}, u32[]{:S(2)}, u32[]{:S(2)}) async-start(bf16[32,96,128]{2,1,0:T(8,128)(2,1)} %bitcast.7), calls=%async_computation.3 | async-start | bytes 1572864 | tf_op jit(solution)/shard_map/exchange_panels/all_to_all | solution.py:131
  102.9 10.8 %copy-start.3 = (f32[2,256,512]{2,1,0:T(8,128)S(1)}, f32[2,256,512]{2,1,0:T(8,128)}, u32[]{:S(2)}) copy-start(f32[2,256,512]{2,1,0:T(8,128)} %param.5) | copy-start | bytes 3145732
  103.0 10.7 %collective-permute-start = (bf16[2,192,768]{2,1,0:T(8,128)(2,1)S(1)}, bf16[2,192,768]{2,1,0:T(8,128)(2,1)S(1)}, u32[]{:S(2)}, u32[]{:S(2)}) collective-permute-start(bf16[2,192,768]{2,1,0:T(8,128)(2,1)S(1)} %pad_maximum_fusion), channel_id=1, source_target_pairs={{0,1},{1,0},{2,3},{3,2},{4,5},{5,4},{6,7},{7,6},{8,9},{9,8},{10,11... | collective-permute-start | bytes 1769480 | tf_op jit(solution)/shard_map/exchange_tp/ppermute | solution.py:143

commit v4 on v3

--- a/solution.py
+++ b/solution.py
@@ -18,7 +18,7 @@
 CHUNKS = 6
 
 
-def note_kernel(ends_ref, columns_ref, out_ref, note_ref, sems):
+def note_kernel(panels_ref, columns_ref, out_ref, ends_ref, note_ref, sems):
     width, rows = columns_ref.shape
     step = width // CHUNKS
     copies = []
@@ -30,6 +30,9 @@
             )
         )
         copies[-1].start()
+    ends = pltpu.make_async_copy(panels_ref, ends_ref, sems.at[CHUNKS + 1])
+    ends.start()
+    ends.wait()
     place = lax.axis_index("fsdp")
     lane = lax.broadcasted_iota(jnp.int32, note_ref.shape, 1)
     note = jnp.zeros(note_ref.shape, jnp.int32)
@@ -50,16 +53,13 @@
     return pl.pallas_call(
         note_kernel,
         out_shape=jax.ShapeDtypeStruct((width, rows + LANES), columns.dtype),
-        in_specs=[
-            pl.BlockSpec(memory_space=pltpu.SMEM),
-            pl.BlockSpec(memory_space=pl.ANY),
-        ],
+        in_specs=[pl.BlockSpec(memory_space=pltpu.HBM)] * 2,
         out_specs=pl.BlockSpec(memory_space=pl.ANY),
         scratch_shapes=[
+            pltpu.SMEM(slot_panels.shape[::-1], slot_panels.dtype),
             pltpu.VMEM((width, LANES), columns.dtype),
-            pltpu.SemaphoreType.DMA((CHUNKS + 1,)),
+            pltpu.SemaphoreType.DMA((CHUNKS + 2,)),
         ],
-        compiler_params=pltpu.CompilerParams(vmem_limit_bytes=16 * 2**20),
         cost_estimate=pl.CostEstimate(flops=0, bytes_accessed=3 * 2**20, transcendentals=0),
     )(slot_panels.T, columns)
 

time: 116 us -> 162 us (1.40)
  Pallas kernels: 2.44 us -> 50.5 us
  local copies, waits for them, and re-layouts: 3.76 us -> 1.67 us
    pallas_call x1, Pallas kernels: 0.77 us -> 48.8 us  [add_note(): pl.pallas_call(note_kernel, out_shape=jax.ShapeDtypeStruct((width, rows +...]
    unnamed x9 -> x5, local copies, waits for them, and re-layouts: 2.19 us -> 0.1 us
where the time goes in v4:
time: 162 us; the launch traced here: 161 us
  blocking collectives  50.8 us (31%)
  Pallas kernels  50.5 us (31%)
  waiting for transfers between devices  28.5 us (18%)
  starting transfers between devices  27.2 us (17%)
  matrix products  1.79 us (1%)
  local copies, waits for them, and re-layouts  1.67 us (1%)
    pallas_call x1, Pallas kernels, add_note(): pl.pallas_call(note_kernel, out_shape=jax.ShapeDtypeStruct((width, rows +...  48.8 us
    all_to_all x1, blocking collectives, body(): lax.all_to_all(noted.reshape(NEAR, SUB, rows + LANES), ('yl', 'zl', 'x'),...  33.8 us
    all_to_all x1, blocking collectives, body(): lax.all_to_all(jnp.concatenate([blocks, note], axis=1), 'yh', 0, 0, tiled...  17 us
    all_to_all x1, waiting for transfers between devices, body(): lax.all_to_all(pieces.reshape(PLANE, PICKS * ZL * SUB, LANES), ('yh', 'yl...  16.7 us
    all_to_all x1, starting transfers between devices, body(): lax.all_to_all(jnp.broadcast_to(summed, (ZL * F, HERE * SUB, LANES)), ('z...  14.2 us
    all_to_all x1, waiting for transfers between devices, body(): lax.all_to_all(jnp.broadcast_to(summed, (ZL * F, HERE * SUB, LANES)), ('z...  10.8 us
    ppermute x1, starting transfers between devices, body(): lax.ppermute(jnp.concatenate([row_half(1 - half), second], axis=2), 'tp',...  9.09 us
    all_to_all x1, starting transfers between devices, body(): lax.all_to_all(pieces.reshape(PLANE, PICKS * ZL * SUB, LANES), ('yh', 'yl...  3.91 us
  transfers between devices with their start and end apart: 3, of which 3 were waited for; matrix products, arithmetic and copies ran while one was open for 1% of the time, Pallas kernels for 0%

profile of v4, /device:TPU:1, one launch (start us, length us, event | category | flops | bytes accessed | tf_op | source)
XLA Modules:
  0.0 161.3 jit_solution(2138278757291550231)
XLA Ops:
  0.0 48.8 %add_note.1 = bf16[192,4224]{1,0:T(8,128)(2,1)} custom-call(s32[2,8]{1,0:T(2,128)} %bitcast.39, bf16[192,4096]{1,0:T(8,128)(2,1)} %bitcast.34), custom_call_target="tpu_custom_call" | custom-call | bytes 3145728 | tf_op jit(solution)/shard_map/add_note/pallas_call | solution.py:53
  48.8 33.8 %all_to_all.20 = bf16[24,8,4224]{2,1,0:T(8,128)(2,1)S(1)} all-to-all(bf16[24,8,4224]{2,1,0:T(8,128)(2,1)} %bitcast.30), channel_id=1, replica_groups=mesh['yh'=4,'yl'=2,'zl'=3,'x'=4,'fsdp'=4,'tp'=2] {'yl','zl','x'}, dimensions={0} | all-to-all | bytes 3244032 | tf_op jit(solution)/shard_map/exchange_near/all_to_all | solution.py:103
  82.7 0.1 convert_element_type.21
  82.8 0.2 convert_reduce_fusion
  83.0 0.1 reshape.54
  83.2 0.1 copy.23
  83.3 17.0 %all_to_all.21 = f32[4,72,128]{2,1,0:T(8,128)S(1)} all-to-all(f32[4,72,128]{2,1,0:T(8,128)S(1)} %pad_maximum_fusion.1), channel_id=1, replica_groups=mesh['yh'=4,'yl'=2,'zl'=3,'x'=4,'fsdp'=4,'tp'=2] {'yh'}, dimensions={0} | all-to-all | bytes 294912 | tf_op jit(solution)/shard_map/exchange_far/all_to_all | solution.py:114
  100.3 0.0 copy-start.1
  100.3 0.7 broadcast_in_dim.43
  101.0 14.2 %all-to-all-start.2 = ((bf16[12,64,128]{2,1,0:T(8,128)(2,1)}), bf16[12,64,128]{2,1,0:T(8,128)(2,1)S(1)}, u32[]{:S(2)}, u32[]{:S(2)}) async-start(bf16[12,64,128]{2,1,0:T(8,128)(2,1)} %broadcast_in_dim.43), calls=%async_computation.2 | async-start | bytes 393216 | tf_op jit(solution)/shard_map/gather_z/all_to_all | solution.py:124
  115.3 0.1 convert_element_type.23
  115.4 0.1 max.12.index_ref
  115.5 10.8 %all-to-all-done.2 = bf16[12,64,128]{2,1,0:T(8,128)(2,1)S(1)} async-done(((bf16[12,64,128]{2,1,0:T(8,128)(2,1)}), bf16[12,64,128]{2,1,0:T(8,128)(2,1)S(1)}, u32[]{:S(2)}, u32[]{:S(2)}) %all-to-all-start.2) | async-done | bytes 196640 | tf_op jit(solution)/shard_map/gather_z/all_to_all | solution.py:124
  126.3 1.7 %pick.1 = bf16[32,4,3,8,128]{4,3,2,1,0:T(8,128)(2,1)} custom-call(s32[128]{0:T(128)S(1)} %max.12.index_ref, bf16[96,8,128]{2,1,0:T(8,128)(2,1)S(1)} %bitcast.29), custom_call_target="tpu_custom_call" | custom-call | bytes 2097152 | tf_op jit(solution)/shard_map/pick/pallas_call | solution.py:80
  128.0 3.9 %all-to-all-start.3 = ((bf16[32,96,128]{2,1,0:T(8,128)(2,1)}), bf16[32,96,128]{2,1,0:T(8,128)(2,1)S(1)}, u32[]{:S(2)}, u32[]{:S(2)}) async-start(bf16[32,96,128]{2,1,0:T(8,128)(2,1)} %bitcast.7), calls=%async_computation.3 | async-start | bytes 1572864 | tf_op jit(solution)/shard_map/exchange_panels/all_to_all | solution.py:131
  131.9 0.0 copy-done.1
  131.9 0.1 select_reduce_fusion.1
  132.1 16.7 %all-to-all-done.3 = bf16[32,96,128]{2,1,0:T(8,128)(2,1)S(1)} async-done(((bf16[32,96,128]{2,1,0:T(8,128)(2,1)}), bf16[32,96,128]{2,1,0:T(8,128)(2,1)S(1)}, u32[]{:S(2)}, u32[]{:S(2)}) %all-to-all-start.3) | async-done | bytes 786464 | tf_op jit(solution)/shard_map/exchange_panels/all_to_all | solution.py:131
  148.7 0.1 fusion.6
  148.9 0.1 copy.21
  149.0 0.1 constant_dynamic-slice_fusion
  149.1 0.0 copy-start
  149.1 9.1 %collective-permute-start = (bf16[2,192,768]{2,1,0:T(8,128)(2,1)S(1)}, bf16[2,192,768]{2,1,0:T(8,128)(2,1)S(1)}, u32[]{:S(2)}, u32[]{:S(2)}) collective-permute-start(bf16[2,192,768]{2,1,0:T(8,128)(2,1)S(1)} %pad_maximum_fusion), channel_id=1, source_target_pairs={{0,1},{1,0},{2,3},{3,2},{4,5},{5,4},{6,7},{7,6},{8,9},{9,8},{10,11... | collective-permute-start | bytes 1769480 | tf_op jit(solution)/shard_map/exchange_tp/ppermute | solution.py:143
  158.2 0.1 pad_add_fusion
  158.3 0.1 slice.28
  158.5 0.4 fusion.7
  158.8 1.0 collective-permute-done
  159.8 0.0 copy-done
  159.8 1.4 fusion.2
  (12 shorter events, 0.3 us)
Async XLA Ops:
  100.3 31.6 %copy-start.1 = (s32[8,2]{0,1:T(2,128)S(1)}, s32[8,2]{0,1:T(2,128)}, u32[]{:S(2)}) copy-start(s32[8,2]{0,1:T(2,128)} %param.4) | copy-start | bytes 196
  101.0 25.3 %all-to-all-start.2 = ((bf16[12,64,128]{2,1,0:T(8,128)(2,1)}), bf16[12,64,128]{2,1,0:T(8,128)(2,1)S(1)}, u32[]{:S(2)}, u32[]{:S(2)}) async-start(bf16[12,64,128]{2,1,0:T(8,128)(2,1)} %broadcast_in_dim.43), calls=%async_computation.2 | async-start | bytes 393216 | tf_op jit(solution)/shard_map/gather_z/all_to_all | solution.py:124
  128.0 20.8 %all-to-all-start.3 = ((bf16[32,96,128]{2,1,0:T(8,128)(2,1)}), bf16[32,96,128]{2,1,0:T(8,128)(2,1)S(1)}, u32[]{:S(2)}, u32[]{:S(2)}) async-start(bf16[32,96,128]{2,1,0:T(8,128)(2,1)} %bitcast.7), calls=%async_computation.3 | async-start | bytes 1572864 | tf_op jit(solution)/shard_map/exchange_panels/all_to_all | solution.py:131
  149.1 10.8 %copy-start = (f32[2,256,512]{2,1,0:T(8,128)S(1)}, f32[2,256,512]{2,1,0:T(8,128)}, u32[]{:S(2)}) copy-start(f32[2,256,512]{2,1,0:T(8,128)} %param.5) | copy-start | bytes 3145732
  149.1 10.7 %collective-permute-start = (bf16[2,192,768]{2,1,0:T(8,128)(2,1)S(1)}, bf16[2,192,768]{2,1,0:T(8,128)(2,1)S(1)}, u32[]{:S(2)}, u32[]{:S(2)}) collective-permute-start(bf16[2,192,768]{2,1,0:T(8,128)(2,1)S(1)} %pad_maximum_fusion), channel_id=1, source_target_pairs={{0,1},{1,0},{2,3},{3,2},{4,5},{5,4},{6,7},{7,6},{8,9},{9,8},{10,11... | collective-permute-start | bytes 1769480 | tf_op jit(solution)/shard_map/exchange_tp/ppermute | solution.py:143

commit v5 on v2

--- a/solution.py
+++ b/solution.py
@@ -7,8 +7,9 @@
 from jax.sharding import PartitionSpec as P
 
 YH, YL, ZL, X, F, T = 4, 2, 3, 4, 4, 2
-NEAR = YL * ZL * X
-PLANE = YH * YL * X
+NEAR = YL * X
+FAR = YH * ZL
+PLANE = YH * NEAR
 TILE = 512
 HERE = 8
 PANELS = HERE * F
@@ -19,10 +20,11 @@
 
 def pick_kernel(index_ref, table_ref, out_ref):
     def step(n, carry):
+        panels = [index_ref[n * PICKS + k] for k in range(PICKS)]
+        found = [[table_ref[z * PANELS + panel] for z in range(ZL)] for panel in panels]
         for k in range(PICKS):
-            panel = index_ref[n * PICKS + k]
             for z in range(ZL):
-                out_ref[n, k, z] = table_ref[z * PANELS + panel]
+                out_ref[n, k, z] = found[k][z]
         return carry
 
     lax.fori_loop(0, PLANE, step, 0, unroll=4)
@@ -49,28 +51,28 @@
     turn = jnp.arange(F * 2, dtype=jnp.int32)[:, None]
     own = [jnp.where(turn == 2 * place + s, slot_panels, 0).sum(0) for s in range(2)]
     own = jnp.concatenate(own)
-    columns = grads[0].T.reshape(NEAR, SUB, rows)
+    columns = grads[0].T.reshape(NEAR, width // NEAR, rows)
     note = jnp.pad(own.astype(grads.dtype), (0, LANES - PICKS))
-    note = jnp.broadcast_to(note, (NEAR, SUB, LANES))
+    note = jnp.broadcast_to(note, (NEAR, width // NEAR, LANES))
     with jax.named_scope("exchange_near"):
         came = lax.all_to_all(
-            jnp.concatenate([columns, note], axis=2), ("yl", "zl", "x"), 0, 0, tiled=True
+            jnp.concatenate([columns, note], axis=2), ("yl", "x"), 0, 0, tiled=True
         )
     near_sum = came[:, :, :rows].astype(jnp.float32).sum(0)
     near_ends = came[:, 0, rows : rows + PICKS].astype(jnp.float32)
 
-    blocks = near_sum.reshape(SUB, HERE, YH, LANES).transpose(2, 1, 0, 3)
-    blocks = blocks.reshape(YH, HERE * SUB, LANES)
+    blocks = near_sum.reshape(ZL, SUB, HERE, YH, LANES).transpose(3, 0, 2, 1, 4)
+    blocks = blocks.reshape(FAR, HERE * SUB, LANES)
     note = jnp.pad(near_ends.reshape(-1), (0, LANES - NEAR * PICKS))
-    note = jnp.broadcast_to(note, (YH, SUB, LANES))
+    note = jnp.broadcast_to(note, (FAR, SUB, LANES))
     with jax.named_scope("exchange_far"):
         came = lax.all_to_all(
-            jnp.concatenate([blocks, note], axis=1), "yh", 0, 0, tiled=True
+            jnp.concatenate([blocks, note], axis=1), ("yh", "zl"), 0, 0, tiled=True
         )
     summed = came[:, : HERE * SUB].sum(0).astype(jnp.bfloat16)
     ends = came[:, HERE * SUB, : NEAR * PICKS].astype(jnp.int32)
-    ends = ends.reshape(YH, YL, ZL, X * PICKS)
-    ends = lax.dynamic_index_in_dim(ends, lax.axis_index("zl"), 2, keepdims=False)
+    ends = ends.reshape(YH, ZL, NEAR * PICKS)
+    ends = lax.dynamic_index_in_dim(ends, lax.axis_index("zl"), 1, keepdims=False)
     ends = jnp.maximum(ends, 0).reshape(PLANE * PICKS)
 
     with jax.named_scope("gather_z"):
@@ -84,17 +86,27 @@
         came = lax.all_to_all(
             pieces.reshape(PLANE, PICKS * ZL * SUB, LANES), ("yh", "yl", "x"), 0, 0, tiled=True
         )
-    came = came.reshape(YH, YL, X, 2, 2, ZL, SUB, LANES)
-    panels = came.transpose(3, 4, 1, 5, 2, 6, 0, 7).reshape(2, 2, width, TILE)
-    first = panels[:, 0].reshape(2, width, T, TILE // T).transpose(2, 0, 1, 3)
-    second = jnp.broadcast_to(panels[:, 1], (T, 2, width, TILE))
+    came = came.reshape(T, YH // T, YL, X, 2, 2, ZL, SUB, LANES)
+    second = came[..., 1, :, :, :].transpose(4, 2, 3, 5, 6, 0, 1, 7).reshape(2, width, TILE)
+    half = lax.axis_index("tp")
+
+    def row_half(place):
+        part = lax.dynamic_index_in_dim(came[..., 0, :, :, :], place, 0, keepdims=False)
+        return part.transpose(3, 1, 2, 4, 5, 0, 6).reshape(2, width, TILE // T)
+
     with jax.named_scope("exchange_tp"):
-        both = lax.all_to_all(
-            jnp.concatenate([first, second], axis=3), "tp", 0, 0, tiled=True
+        other = lax.ppermute(
+            jnp.concatenate([row_half(1 - half), second], axis=2), "tp", [(0, 1), (1, 0)]
         )
-    first = both[..., : TILE // T]
-    second = both[..., TILE // T :]
-    product = jnp.einsum("tsca,tscb->sab", first, second, preferred_element_type=jnp.float32)
+    product = jnp.einsum(
+        "sca,scb->sab", row_half(half), second, preferred_element_type=jnp.float32
+    )
+    product = product + jnp.einsum(
+        "sca,scb->sab",
+        other[..., : TILE // T],
+        other[..., TILE // T :],
+        preferred_element_type=jnp.float32,
+    )
     valid = own[0::2] >= 0
     product = jnp.where(valid[:, None, None], product, 0.0)
     return 0.9 * factor_old + 0.1 * product

time: 116 us -> 116 us (level)
  blocking collectives: 62.1 us -> 48.2 us
  starting transfers between devices: 18.1 us -> 28.1 us
  waiting for transfers between devices: 27.6 us -> 31 us
    all_to_all x3 -> x2, blocking collectives: 62.1 us -> 48.2 us  [the longest x1 28.1 us: body(): lax.all_to_all(jnp.concatenate([blocks, note], axis=1), ('yh', 'zl'), 0,...]
    ppermute x0 -> x1, starting transfers between devices: none -> 7.09 us  [body(): lax.ppermute(jnp.concatenate([row_half(1 - half), second], axis=2), 'tp',...]
    all_to_all x1, waiting for transfers between devices: 16.7 us -> 19.1 us  [body(): lax.all_to_all(pieces.reshape(PLANE, PICKS * ZL * SUB, LANES), ('yh', 'yl...]
    all_to_all x1, starting transfers between devices: 14.2 us -> 15.9 us  [body(): lax.all_to_all(jnp.broadcast_to(summed, (ZL * F, HERE * SUB, LANES)), ('z...]
    all_to_all x1, starting transfers between devices: 3.91 us -> 5.12 us  [body(): lax.all_to_all(pieces.reshape(PLANE, PICKS * ZL * SUB, LANES), ('yh', 'yl...]
  transfers between devices with their start and end apart: 2 -> 3, of which waited for: 2 -> 3; matrix products, arithmetic and copies ran while one was open for 0% -> 1% of each run, Pallas kernels for 0% -> 0%
where the time goes in v5:
time: 116 us
  blocking collectives  48.2 us (42%)
  waiting for transfers between devices  31 us (27%)
  starting transfers between devices  28.1 us (24%)
  other arithmetic  2.98 us (3%)
  local copies, waits for them, and re-layouts  1.83 us (2%)
  matrix products  1.79 us (2%)
  Pallas kernels  1.67 us (1%)
    all_to_all x1, blocking collectives, body(): lax.all_to_all(jnp.concatenate([blocks, note], axis=1), ('yh', 'zl'), 0,...  28.1 us
    all_to_all x1, blocking collectives, body(): lax.all_to_all(jnp.concatenate([columns, note], axis=2), ('yl', 'x'), 0,...  20.2 us
    all_to_all x1, waiting for transfers between devices, body(): lax.all_to_all(pieces.reshape(PLANE, PICKS * ZL * SUB, LANES), ('yh', 'yl...  19.1 us
    all_to_all x1, starting transfers between devices, body(): lax.all_to_all(jnp.broadcast_to(summed, (ZL * F, HERE * SUB, LANES)), ('z...  15.9 us
    all_to_all x1, waiting for transfers between devices, body(): lax.all_to_all(jnp.broadcast_to(summed, (ZL * F, HERE * SUB, LANES)), ('z...  10.8 us
    ppermute x1, starting transfers between devices, body(): lax.ppermute(jnp.concatenate([row_half(1 - half), second], axis=2), 'tp',...  7.09 us
    all_to_all x1, starting transfers between devices, body(): lax.all_to_all(pieces.reshape(PLANE, PICKS * ZL * SUB, LANES), ('yh', 'yl...  5.12 us
  transfers between devices with their start and end apart: 3, of which 3 were waited for; matrix products, arithmetic and copies ran while one was open for 1% of the time, Pallas kernels for 0%

profile of v5, /device:TPU:1, one launch (start us, length us, event | category | flops | bytes accessed | tf_op | source)
XLA Modules:
  0.0 115.8 jit_solution(16113963756144274005)
XLA Ops:
  0.0 0.8 select_reduce_fusion.1
  0.8 0.1 fusion.7
  0.9 1.7 %pad_maximum_fusion = bf16[8,24,4224]{2,1,0:T(8,128)(2,1)S(1)} fusion(bf16[8,24,4096]{2,1,0:T(8,128)(2,1)} %bitcast.33, bf16[4224]{0:T(1024)(128)(2,1)S(1)} %fusion.5), kind=kLoop, calls=%fused_computation.1 | loop fusion | flops 3244032 | bytes 3203328 | tf_op jit(solution)/shard_map/exchange_near/concatenate | solution.py:59
  2.6 20.2 %all_to_all.20 = bf16[8,24,4224]{2,1,0:T(8,128)(2,1)S(1)} all-to-all(bf16[8,24,4224]{2,1,0:T(8,128)(2,1)S(1)} %pad_maximum_fusion), channel_id=1, replica_groups=mesh['yh'=4,'yl'=2,'zl'=3,'x'=4,'fsdp'=4,'tp'=2] {'yl','x'}, dimensions={0} | all-to-all | bytes 3244032 | tf_op jit(solution)/shard_map/exchange_near/all_to_all | solution.py:58
  22.8 0.2 convert_reduce_fusion
  23.0 0.3 reshape.54
  23.3 0.2 copy.17
  23.5 0.1 convert_element_type.27
  23.7 28.1 %all_to_all.21 = f32[12,72,128]{2,1,0:T(8,128)S(1)} all-to-all(f32[12,72,128]{2,1,0:T(8,128)S(1)} %pad_maximum_fusion.2), channel_id=1, replica_groups=mesh['yh'=4,'yl'=2,'zl'=3,'x'=4,'fsdp'=4,'tp'=2] {'yh','zl'}, dimensions={0} | all-to-all | bytes 884736 | tf_op jit(solution)/shard_map/exchange_far/all_to_all | solution.py:69
  51.8 0.7 broadcast_in_dim.47
  52.5 15.9 %all-to-all-start.2 = ((bf16[12,64,128]{2,1,0:T(8,128)(2,1)}), bf16[12,64,128]{2,1,0:T(8,128)(2,1)S(1)}, u32[]{:S(2)}, u32[]{:S(2)}) async-start(bf16[12,64,128]{2,1,0:T(8,128)(2,1)} %broadcast_in_dim.47), calls=%async_computation.2 | async-start | bytes 393216 | tf_op jit(solution)/shard_map/gather_z/all_to_all | solution.py:79
  68.4 0.1 max.12.index_ref
  68.5 10.8 %all-to-all-done.2 = bf16[12,64,128]{2,1,0:T(8,128)(2,1)S(1)} async-done(((bf16[12,64,128]{2,1,0:T(8,128)(2,1)}), bf16[12,64,128]{2,1,0:T(8,128)(2,1)S(1)}, u32[]{:S(2)}, u32[]{:S(2)}) %all-to-all-start.2) | async-done | bytes 196640 | tf_op jit(solution)/shard_map/gather_z/all_to_all | solution.py:79
  79.3 1.7 %pick.1 = bf16[32,4,3,8,128]{4,3,2,1,0:T(8,128)(2,1)} custom-call(s32[128]{0:T(128)S(1)} %max.12.index_ref, bf16[96,8,128]{2,1,0:T(8,128)(2,1)S(1)} %bitcast.27), custom_call_target="tpu_custom_call" | custom-call | bytes 2097152 | tf_op jit(solution)/shard_map/pick/pallas_call | solution.py:34
  81.0 5.1 %all-to-all-start.3 = ((bf16[32,96,128]{2,1,0:T(8,128)(2,1)}), bf16[32,96,128]{2,1,0:T(8,128)(2,1)S(1)}, u32[]{:S(2)}, u32[]{:S(2)}) async-start(bf16[32,96,128]{2,1,0:T(8,128)(2,1)} %bitcast.6), calls=%async_computation.3 | async-start | bytes 1572864 | tf_op jit(solution)/shard_map/exchange_panels/all_to_all | solution.py:86
  86.1 19.1 %all-to-all-done.3 = bf16[32,96,128]{2,1,0:T(8,128)(2,1)S(1)} async-done(((bf16[32,96,128]{2,1,0:T(8,128)(2,1)}), bf16[32,96,128]{2,1,0:T(8,128)(2,1)S(1)}, u32[]{:S(2)}, u32[]{:S(2)}) %all-to-all-start.3) | async-done | bytes 786464 | tf_op jit(solution)/shard_map/exchange_panels/all_to_all | solution.py:86
  105.3 0.1 fusion.8
  105.4 0.1 constant_dynamic-slice_fusion
  105.5 0.1 copy.22
  105.6 0.0 copy-start
  105.6 7.1 %collective-permute-start = (bf16[2,192,768]{2,1,0:T(8,128)(2,1)S(1)}, bf16[2,192,768]{2,1,0:T(8,128)(2,1)S(1)}, u32[]{:S(2)}, u32[]{:S(2)}) collective-permute-start(bf16[2,192,768]{2,1,0:T(8,128)(2,1)S(1)} %pad_maximum_fusion.1), channel_id=1, source_target_pairs={{0,1},{1,0},{2,3},{3,2},{4,5},{5,4},{6,7},{7,6},{8,9},{9,8},{10,11... | collective-permute-start | bytes 1769480 | tf_op jit(solution)/shard_map/exchange_tp/ppermute | solution.py:98
  112.7 0.1 slice.28
  112.9 0.4 fusion.9
  113.2 1.1 collective-permute-done
  114.3 0.0 copy-done
  114.3 1.4 %fusion.2 = f32[2,256,512]{2,1,0:T(8,128)} fusion(f32[2,256,512]{2,1,0:T(8,128)S(1)} %fusion.9, f32[2,256,512]{2,1,0:T(8,128)S(1)} %copy-done, pred[2]{0:T(512)(128)(4,1)S(1)} %broadcast_compare_fusion, bf16[2,192,768]{2,1,0:T(8,128)(2,1)S(1)} %collective-permute-done), kind=kOutput, calls=%fused_computation.5 | convolution fusion | flops 101974016 | bytes 3735554 | tf_op jit(solution)/shard_map/sca,scb->sab/dot_general | solution.py:104
  (14 shorter events, 0.3 us)
Async XLA Ops:
  52.5 26.9 %all-to-all-start.2 = ((bf16[12,64,128]{2,1,0:T(8,128)(2,1)}), bf16[12,64,128]{2,1,0:T(8,128)(2,1)S(1)}, u32[]{:S(2)}, u32[]{:S(2)}) async-start(bf16[12,64,128]{2,1,0:T(8,128)(2,1)} %broadcast_in_dim.47), calls=%async_computation.2 | async-start | bytes 393216 | tf_op jit(solution)/shard_map/gather_z/all_to_all | solution.py:79
  81.0 24.3 %all-to-all-start.3 = ((bf16[32,96,128]{2,1,0:T(8,128)(2,1)}), bf16[32,96,128]{2,1,0:T(8,128)(2,1)S(1)}, u32[]{:S(2)}, u32[]{:S(2)}) async-start(bf16[32,96,128]{2,1,0:T(8,128)(2,1)} %bitcast.6), calls=%async_computation.3 | async-start | bytes 1572864 | tf_op jit(solution)/shard_map/exchange_panels/all_to_all | solution.py:86
  105.6 8.8 %copy-start = (f32[2,256,512]{2,1,0:T(8,128)S(1)}, f32[2,256,512]{2,1,0:T(8,128)}, u32[]{:S(2)}) copy-start(f32[2,256,512]{2,1,0:T(8,128)} %param.5) | copy-start | bytes 3145732
  105.6 8.7 %collective-permute-start = (bf16[2,192,768]{2,1,0:T(8,128)(2,1)S(1)}, bf16[2,192,768]{2,1,0:T(8,128)(2,1)S(1)}, u32[]{:S(2)}, u32[]{:S(2)}) collective-permute-start(bf16[2,192,768]{2,1,0:T(8,128)(2,1)S(1)} %pad_maximum_fusion.1), channel_id=1, source_target_pairs={{0,1},{1,0},{2,3},{3,2},{4,5},{5,4},{6,7},{7,6},{8,9},{9,8},{10,11... | collective-permute-start | bytes 1769480 | tf_op jit(solution)/shard_map/exchange_tp/ppermute | solution.py:98

commit v6 on v5

--- a/solution.py
+++ b/solution.py
@@ -7,38 +7,41 @@
 from jax.sharding import PartitionSpec as P
 
 YH, YL, ZL, X, F, T = 4, 2, 3, 4, 4, 2
-NEAR = YL * X
-FAR = YH * ZL
-PLANE = YH * NEAR
+NEAR = YL * ZL * X
+PLANE = YH * YL * X
 TILE = 512
 HERE = 8
 PANELS = HERE * F
 PICKS = 4
 LANES = 128
 SUB = 8
+PART = 8
 
 
 def pick_kernel(index_ref, table_ref, out_ref):
+    first = pl.program_id(0) * PART
+
     def step(n, carry):
-        panels = [index_ref[n * PICKS + k] for k in range(PICKS)]
+        panels = [index_ref[(first + n) * PICKS + k] for k in range(PICKS)]
         found = [[table_ref[z * PANELS + panel] for z in range(ZL)] for panel in panels]
         for k in range(PICKS):
             for z in range(ZL):
                 out_ref[n, k, z] = found[k][z]
         return carry
 
-    lax.fori_loop(0, PLANE, step, 0, unroll=4)
+    lax.fori_loop(0, PART, step, 0, unroll=4)
 
 
 def pick_pieces(index, table):
     return pl.pallas_call(
         pick_kernel,
         out_shape=jax.ShapeDtypeStruct((PLANE, PICKS, ZL, SUB, LANES), table.dtype),
+        grid=(PLANE // PART,),
         in_specs=[
             pl.BlockSpec(memory_space=pltpu.SMEM),
             pl.BlockSpec(memory_space=pltpu.VMEM),
         ],
-        out_specs=pl.BlockSpec(memory_space=pltpu.VMEM),
+        out_specs=pl.BlockSpec((PART, PICKS, ZL, SUB, LANES), lambda n: (n, 0, 0, 0, 0)),
         compiler_params=pltpu.CompilerParams(vmem_limit_bytes=16 * 2**20),
         cost_estimate=pl.CostEstimate(flops=0, bytes_accessed=2 * 2**20, transcendentals=0),
     )(index, table)
@@ -56,23 +59,23 @@
     note = jnp.broadcast_to(note, (NEAR, width // NEAR, LANES))
     with jax.named_scope("exchange_near"):
         came = lax.all_to_all(
-            jnp.concatenate([columns, note], axis=2), ("yl", "x"), 0, 0, tiled=True
+            jnp.concatenate([columns, note], axis=2), ("yl", "zl", "x"), 0, 0, tiled=True
         )
     near_sum = came[:, :, :rows].astype(jnp.float32).sum(0)
     near_ends = came[:, 0, rows : rows + PICKS].astype(jnp.float32)
 
-    blocks = near_sum.reshape(ZL, SUB, HERE, YH, LANES).transpose(3, 0, 2, 1, 4)
-    blocks = blocks.reshape(FAR, HERE * SUB, LANES)
+    blocks = near_sum.reshape(SUB, HERE, YH, LANES).transpose(2, 1, 0, 3)
+    blocks = blocks.reshape(YH, HERE * SUB, LANES)
     note = jnp.pad(near_ends.reshape(-1), (0, LANES - NEAR * PICKS))
-    note = jnp.broadcast_to(note, (FAR, SUB, LANES))
+    note = jnp.broadcast_to(note, (YH, SUB, LANES))
     with jax.named_scope("exchange_far"):
         came = lax.all_to_all(
-            jnp.concatenate([blocks, note], axis=1), ("yh", "zl"), 0, 0, tiled=True
+            jnp.concatenate([blocks, note], axis=1), "yh", 0, 0, tiled=True
         )
     summed = came[:, : HERE * SUB].sum(0).astype(jnp.bfloat16)
     ends = came[:, HERE * SUB, : NEAR * PICKS].astype(jnp.int32)
-    ends = ends.reshape(YH, ZL, NEAR * PICKS)
-    ends = lax.dynamic_index_in_dim(ends, lax.axis_index("zl"), 1, keepdims=False)
+    ends = ends.reshape(YH, YL, ZL, X * PICKS)
+    ends = lax.dynamic_index_in_dim(ends, lax.axis_index("zl"), 2, keepdims=False)
     ends = jnp.maximum(ends, 0).reshape(PLANE * PICKS)
 
     with jax.named_scope("gather_z"):
@@ -87,12 +90,12 @@
             pieces.reshape(PLANE, PICKS * ZL * SUB, LANES), ("yh", "yl", "x"), 0, 0, tiled=True
         )
     came = came.reshape(T, YH // T, YL, X, 2, 2, ZL, SUB, LANES)
-    second = came[..., 1, :, :, :].transpose(4, 2, 3, 5, 6, 0, 1, 7).reshape(2, width, TILE)
+    second = came[..., 1, :, :, :].transpose(4, 2, 5, 3, 6, 0, 1, 7).reshape(2, width, TILE)
     half = lax.axis_index("tp")
 
     def row_half(place):
         part = lax.dynamic_index_in_dim(came[..., 0, :, :, :], place, 0, keepdims=False)
-        return part.transpose(3, 1, 2, 4, 5, 0, 6).reshape(2, width, TILE // T)
+        return part.transpose(3, 1, 4, 2, 5, 0, 6).reshape(2, width, TILE // T)
 
     with jax.named_scope("exchange_tp"):
         other = lax.ppermute(

time: 116 us -> 116 us (level)
  blocking collectives: 48.2 us -> 50.6 us
  waiting for transfers between devices: 31 us -> 28.8 us
    all_to_all x2, blocking collectives: 48.2 us -> 50.6 us  [the longest x1 34.5 us: body(): lax.all_to_all(jnp.concatenate([columns, note], axis=2), ('yl', 'zl', 'x'...]
    all_to_all x1, waiting for transfers between devices: 19.1 us -> 16.8 us  [body(): lax.all_to_all(pieces.reshape(PLANE, PICKS * ZL * SUB, LANES), ('yh', 'yl...]
    ppermute x1, starting transfers between devices: 7.09 us -> 9.09 us  [body(): lax.ppermute(jnp.concatenate([row_half(1 - half), second], axis=2), 'tp',...]
    all_to_all x1, starting transfers between devices: 15.9 us -> 14.2 us  [body(): lax.all_to_all(jnp.broadcast_to(summed, (ZL * F, HERE * SUB, LANES)), ('z...]
    all_to_all x1, starting transfers between devices: 5.12 us -> 3.91 us  [body(): lax.all_to_all(pieces.reshape(PLANE, PICKS * ZL * SUB, LANES), ('yh', 'yl...]
where the time goes in v6:
time: 116 us; the launch traced here: 115 us
  blocking collectives  50.6 us (44%)
  waiting for transfers between devices  28.8 us (25%)
  starting transfers between devices  27.2 us (23%)
  other arithmetic  2.95 us (3%)
  Pallas kernels  2.12 us (2%)
  matrix products  1.79 us (2%)
  local copies, waits for them, and re-layouts  1.66 us (1%)
    all_to_all x1, blocking collectives, body(): lax.all_to_all(jnp.concatenate([columns, note], axis=2), ('yl', 'zl', 'x'...  34.5 us
    all_to_all x1, waiting for transfers between devices, body(): lax.all_to_all(pieces.reshape(PLANE, PICKS * ZL * SUB, LANES), ('yh', 'yl...  16.8 us
    all_to_all x1, blocking collectives, body(): lax.all_to_all(jnp.concatenate([blocks, note], axis=1), 'yh', 0, 0, tiled...  16.2 us
    all_to_all x1, starting transfers between devices, body(): lax.all_to_all(jnp.broadcast_to(summed, (ZL * F, HERE * SUB, LANES)), ('z...  14.2 us
    all_to_all x1, waiting for transfers between devices, body(): lax.all_to_all(jnp.broadcast_to(summed, (ZL * F, HERE * SUB, LANES)), ('z...  10.8 us
    ppermute x1, starting transfers between devices, body(): lax.ppermute(jnp.concatenate([row_half(1 - half), second], axis=2), 'tp',...  9.09 us
    all_to_all x1, starting transfers between devices, body(): lax.all_to_all(pieces.reshape(PLANE, PICKS * ZL * SUB, LANES), ('yh', 'yl...  3.91 us
  transfers between devices with their start and end apart: 3, of which 3 were waited for; matrix products, arithmetic and copies ran while one was open for 1% of the time, Pallas kernels for 0%

profile of v6, /device:TPU:1, one launch (start us, length us, event | category | flops | bytes accessed | tf_op | source)
XLA Modules:
  0.0 115.3 jit_solution(11062733856064624067)
XLA Ops:
  0.0 0.8 select_reduce_fusion.1
  0.8 0.1 fusion.7
  0.9 1.7 %pad_maximum_fusion = bf16[24,8,4224]{2,1,0:T(8,128)(2,1)S(1)} fusion(bf16[24,8,4096]{2,1,0:T(8,128)(2,1)} %bitcast.33, bf16[4224]{0:T(1024)(128)(2,1)S(1)} %fusion.5), kind=kLoop, calls=%fused_computation.1 | loop fusion | flops 3244032 | bytes 3203328 | tf_op jit(solution)/shard_map/exchange_near/concatenate | solution.py:62
  2.6 34.5 %all_to_all.20 = bf16[24,8,4224]{2,1,0:T(8,128)(2,1)S(1)} all-to-all(bf16[24,8,4224]{2,1,0:T(8,128)(2,1)S(1)} %pad_maximum_fusion), channel_id=1, replica_groups=mesh['yh'=4,'yl'=2,'zl'=3,'x'=4,'fsdp'=4,'tp'=2] {'yl','zl','x'}, dimensions={0} | all-to-all | bytes 3244032 | tf_op jit(solution)/shard_map/exchange_near/all_to_all | solution.py:61
  37.1 0.2 convert_reduce_fusion
  37.3 0.1 reshape.54
  37.4 0.1 copy.23
  37.5 0.1 convert_element_type.27
  37.7 16.2 %all_to_all.21 = f32[4,72,128]{2,1,0:T(8,128)S(1)} all-to-all(f32[4,72,128]{2,1,0:T(8,128)S(1)} %pad_maximum_fusion.2), channel_id=1, replica_groups=mesh['yh'=4,'yl'=2,'zl'=3,'x'=4,'fsdp'=4,'tp'=2] {'yh'}, dimensions={0} | all-to-all | bytes 294912 | tf_op jit(solution)/shard_map/exchange_far/all_to_all | solution.py:72
  53.9 0.7 broadcast_in_dim.47
  54.6 14.2 %all-to-all-start.2 = ((bf16[12,64,128]{2,1,0:T(8,128)(2,1)}), bf16[12,64,128]{2,1,0:T(8,128)(2,1)S(1)}, u32[]{:S(2)}, u32[]{:S(2)}) async-start(bf16[12,64,128]{2,1,0:T(8,128)(2,1)} %broadcast_in_dim.47), calls=%async_computation.2 | async-start | bytes 393216 | tf_op jit(solution)/shard_map/gather_z/all_to_all | solution.py:82
  68.8 0.1 convert_element_type.29
  69.0 0.1 max.12.index_ref
  69.0 10.8 %all-to-all-done.2 = bf16[12,64,128]{2,1,0:T(8,128)(2,1)S(1)} async-done(((bf16[12,64,128]{2,1,0:T(8,128)(2,1)}), bf16[12,64,128]{2,1,0:T(8,128)(2,1)S(1)}, u32[]{:S(2)}, u32[]{:S(2)}) %all-to-all-start.2) | async-done | bytes 196640 | tf_op jit(solution)/shard_map/gather_z/all_to_all | solution.py:82
  79.9 2.1 %pick.1 = bf16[32,4,3,8,128]{4,3,2,1,0:T(8,128)(2,1)} custom-call(s32[128]{0:T(128)S(1)} %max.12.index_ref, bf16[96,8,128]{2,1,0:T(8,128)(2,1)S(1)} %bitcast.29), custom_call_target="tpu_custom_call" | custom-call | bytes 2097152 | tf_op jit(solution)/shard_map/pick/pallas_call | solution.py:36
  82.0 3.9 %all-to-all-start.3 = ((bf16[32,96,128]{2,1,0:T(8,128)(2,1)}), bf16[32,96,128]{2,1,0:T(8,128)(2,1)S(1)}, u32[]{:S(2)}, u32[]{:S(2)}) async-start(bf16[32,96,128]{2,1,0:T(8,128)(2,1)} %bitcast.6), calls=%async_computation.3 | async-start | bytes 1572864 | tf_op jit(solution)/shard_map/exchange_panels/all_to_all | solution.py:89
  85.9 16.8 %all-to-all-done.3 = bf16[32,96,128]{2,1,0:T(8,128)(2,1)S(1)} async-done(((bf16[32,96,128]{2,1,0:T(8,128)(2,1)}), bf16[32,96,128]{2,1,0:T(8,128)(2,1)S(1)}, u32[]{:S(2)}, u32[]{:S(2)}) %all-to-all-start.3) | async-done | bytes 786464 | tf_op jit(solution)/shard_map/exchange_panels/all_to_all | solution.py:89
  102.8 0.1 fusion.8
  102.9 0.1 constant_dynamic-slice_fusion
  103.0 0.1 copy.21
  103.1 0.0 copy-start
  103.1 9.1 %collective-permute-start = (bf16[2,192,768]{2,1,0:T(8,128)(2,1)S(1)}, bf16[2,192,768]{2,1,0:T(8,128)(2,1)S(1)}, u32[]{:S(2)}, u32[]{:S(2)}) collective-permute-start(bf16[2,192,768]{2,1,0:T(8,128)(2,1)S(1)} %pad_maximum_fusion.1), channel_id=1, source_target_pairs={{0,1},{1,0},{2,3},{3,2},{4,5},{5,4},{6,7},{7,6},{8,9},{9,8},{10,11... | collective-permute-start | bytes 1769480 | tf_op jit(solution)/shard_map/exchange_tp/ppermute | solution.py:101
  112.2 0.1 slice.28
  112.4 0.4 fusion.9
  112.7 1.1 collective-permute-done
  113.8 0.0 copy-done
  113.9 1.4 %fusion.2 = f32[2,256,512]{2,1,0:T(8,128)} fusion(f32[2,256,512]{2,1,0:T(8,128)S(1)} %fusion.9, f32[2,256,512]{2,1,0:T(8,128)S(1)} %copy-done, pred[2]{0:T(512)(128)(4,1)S(1)} %broadcast_compare_fusion, bf16[2,192,768]{2,1,0:T(8,128)(2,1)S(1)} %collective-permute-done), kind=kOutput, calls=%fused_computation.5 | convolution fusion | flops 101974016 | bytes 3735554 | tf_op jit(solution)/shard_map/sca,scb->sab/dot_general | solution.py:107
  (13 shorter events, 0.3 us)
Async XLA Ops:
  54.6 25.3 %all-to-all-start.2 = ((bf16[12,64,128]{2,1,0:T(8,128)(2,1)}), bf16[12,64,128]{2,1,0:T(8,128)(2,1)S(1)}, u32[]{:S(2)}, u32[]{:S(2)}) async-start(bf16[12,64,128]{2,1,0:T(8,128)(2,1)} %broadcast_in_dim.47), calls=%async_computation.2 | async-start | bytes 393216 | tf_op jit(solution)/shard_map/gather_z/all_to_all | solution.py:82
  82.0 20.8 %all-to-all-start.3 = ((bf16[32,96,128]{2,1,0:T(8,128)(2,1)}), bf16[32,96,128]{2,1,0:T(8,128)(2,1)S(1)}, u32[]{:S(2)}, u32[]{:S(2)}) async-start(bf16[32,96,128]{2,1,0:T(8,128)(2,1)} %bitcast.6), calls=%async_computation.3 | async-start | bytes 1572864 | tf_op jit(solution)/shard_map/exchange_panels/all_to_all | solution.py:89
  103.1 10.8 %copy-start = (f32[2,256,512]{2,1,0:T(8,128)S(1)}, f32[2,256,512]{2,1,0:T(8,128)}, u32[]{:S(2)}) copy-start(f32[2,256,512]{2,1,0:T(8,128)} %param.5) | copy-start | bytes 3145732
  103.1 10.7 %collective-permute-start = (bf16[2,192,768]{2,1,0:T(8,128)(2,1)S(1)}, bf16[2,192,768]{2,1,0:T(8,128)(2,1)S(1)}, u32[]{:S(2)}, u32[]{:S(2)}) collective-permute-start(bf16[2,192,768]{2,1,0:T(8,128)(2,1)S(1)} %pad_maximum_fusion.1), channel_id=1, source_target_pairs={{0,1},{1,0},{2,3},{3,2},{4,5},{5,4},{6,7},{7,6},{8,9},{9,8},{10,11... | collective-permute-start | bytes 1769480 | tf_op jit(solution)/shard_map/exchange_tp/ppermute | solution.py:101

commit v7 on v6

--- a/solution.py
+++ b/solution.py
@@ -15,33 +15,29 @@
 PICKS = 4
 LANES = 128
 SUB = 8
-PART = 8
 
 
 def pick_kernel(index_ref, table_ref, out_ref):
-    first = pl.program_id(0) * PART
-
     def step(n, carry):
-        panels = [index_ref[(first + n) * PICKS + k] for k in range(PICKS)]
+        panels = [index_ref[n * PICKS + k] for k in range(PICKS)]
         found = [[table_ref[z * PANELS + panel] for z in range(ZL)] for panel in panels]
         for k in range(PICKS):
             for z in range(ZL):
                 out_ref[n, k, z] = found[k][z]
         return carry
 
-    lax.fori_loop(0, PART, step, 0, unroll=4)
+    lax.fori_loop(0, PLANE, step, 0, unroll=4)
 
 
 def pick_pieces(index, table):
     return pl.pallas_call(
         pick_kernel,
         out_shape=jax.ShapeDtypeStruct((PLANE, PICKS, ZL, SUB, LANES), table.dtype),
-        grid=(PLANE // PART,),
         in_specs=[
             pl.BlockSpec(memory_space=pltpu.SMEM),
             pl.BlockSpec(memory_space=pltpu.VMEM),
         ],
-        out_specs=pl.BlockSpec((PART, PICKS, ZL, SUB, LANES), lambda n: (n, 0, 0, 0, 0)),
+        out_specs=pl.BlockSpec(memory_space=pltpu.VMEM),
         compiler_params=pltpu.CompilerParams(vmem_limit_bytes=16 * 2**20),
         cost_estimate=pl.CostEstimate(flops=0, bytes_accessed=2 * 2**20, transcendentals=0),
     )(index, table)

time: 116 us -> 115 us (level)
  no operation moved by 1% of the time
where the time goes in v7:
time: 115 us
  blocking collectives  50.6 us (44%)
  waiting for transfers between devices  28.8 us (25%)
  starting transfers between devices  27.2 us (24%)
  other arithmetic  2.95 us (3%)
  matrix products  1.79 us (2%)
  Pallas kernels  1.67 us (1%)
  local copies, waits for them, and re-layouts  1.66 us (1%)
    all_to_all x1, blocking collectives, body(): lax.all_to_all(jnp.concatenate([columns, note], axis=2), ('yl', 'zl', 'x'...  34.5 us
    all_to_all x1, waiting for transfers between devices, body(): lax.all_to_all(pieces.reshape(PLANE, PICKS * ZL * SUB, LANES), ('yh', 'yl...  16.8 us
    all_to_all x1, blocking collectives, body(): lax.all_to_all(jnp.concatenate([blocks, note], axis=1), 'yh', 0, 0, tiled...  16.2 us
    all_to_all x1, starting transfers between devices, body(): lax.all_to_all(jnp.broadcast_to(summed, (ZL * F, HERE * SUB, LANES)), ('z...  14.2 us
    all_to_all x1, waiting for transfers between devices, body(): lax.all_to_all(jnp.broadcast_to(summed, (ZL * F, HERE * SUB, LANES)), ('z...  10.8 us
    ppermute x1, starting transfers between devices, body(): lax.ppermute(jnp.concatenate([row_half(1 - half), second], axis=2), 'tp',...  9.09 us
    all_to_all x1, starting transfers between devices, body(): lax.all_to_all(pieces.reshape(PLANE, PICKS * ZL * SUB, LANES), ('yh', 'yl...  3.91 us
  transfers between devices with their start and end apart: 3, of which 3 were waited for; matrix products, arithmetic and copies ran while one was open for 1% of the time, Pallas kernels for 0%

profile of v7, /device:TPU:1, one launch (start us, length us, event | category | flops | bytes accessed | tf_op | source)
XLA Modules:
  0.0 114.8 jit_solution(17982460680004712301)
XLA Ops:
  0.0 0.8 select_reduce_fusion.1
  0.8 0.1 fusion.7
  0.9 1.7 %pad_maximum_fusion = bf16[24,8,4224]{2,1,0:T(8,128)(2,1)S(1)} fusion(bf16[24,8,4096]{2,1,0:T(8,128)(2,1)} %bitcast.33, bf16[4224]{0:T(1024)(128)(2,1)S(1)} %fusion.5), kind=kLoop, calls=%fused_computation.1 | loop fusion | flops 3244032 | bytes 3203328 | tf_op jit(solution)/shard_map/exchange_near/concatenate | solution.py:58
  2.6 34.5 %all_to_all.20 = bf16[24,8,4224]{2,1,0:T(8,128)(2,1)S(1)} all-to-all(bf16[24,8,4224]{2,1,0:T(8,128)(2,1)S(1)} %pad_maximum_fusion), channel_id=1, replica_groups=mesh['yh'=4,'yl'=2,'zl'=3,'x'=4,'fsdp'=4,'tp'=2] {'yl','zl','x'}, dimensions={0} | all-to-all | bytes 3244032 | tf_op jit(solution)/shard_map/exchange_near/all_to_all | solution.py:57
  37.1 0.2 convert_reduce_fusion
  37.3 0.1 reshape.54
  37.4 0.1 copy.23
  37.5 0.1 convert_element_type.27
  37.7 16.2 %all_to_all.21 = f32[4,72,128]{2,1,0:T(8,128)S(1)} all-to-all(f32[4,72,128]{2,1,0:T(8,128)S(1)} %pad_maximum_fusion.2), channel_id=1, replica_groups=mesh['yh'=4,'yl'=2,'zl'=3,'x'=4,'fsdp'=4,'tp'=2] {'yh'}, dimensions={0} | all-to-all | bytes 294912 | tf_op jit(solution)/shard_map/exchange_far/all_to_all | solution.py:68
  53.9 0.7 broadcast_in_dim.47
  54.6 14.2 %all-to-all-start.2 = ((bf16[12,64,128]{2,1,0:T(8,128)(2,1)}), bf16[12,64,128]{2,1,0:T(8,128)(2,1)S(1)}, u32[]{:S(2)}, u32[]{:S(2)}) async-start(bf16[12,64,128]{2,1,0:T(8,128)(2,1)} %broadcast_in_dim.47), calls=%async_computation.2 | async-start | bytes 393216 | tf_op jit(solution)/shard_map/gather_z/all_to_all | solution.py:78
  68.8 0.1 convert_element_type.29
  69.0 0.1 max.12.index_ref
  69.0 10.8 %all-to-all-done.2 = bf16[12,64,128]{2,1,0:T(8,128)(2,1)S(1)} async-done(((bf16[12,64,128]{2,1,0:T(8,128)(2,1)}), bf16[12,64,128]{2,1,0:T(8,128)(2,1)S(1)}, u32[]{:S(2)}, u32[]{:S(2)}) %all-to-all-start.2) | async-done | bytes 196640 | tf_op jit(solution)/shard_map/gather_z/all_to_all | solution.py:78
  79.9 1.7 %pick.1 = bf16[32,4,3,8,128]{4,3,2,1,0:T(8,128)(2,1)} custom-call(s32[128]{0:T(128)S(1)} %max.12.index_ref, bf16[96,8,128]{2,1,0:T(8,128)(2,1)S(1)} %bitcast.29), custom_call_target="tpu_custom_call" | custom-call | bytes 2097152 | tf_op jit(solution)/shard_map/pick/pallas_call | solution.py:33
  81.5 3.9 %all-to-all-start.3 = ((bf16[32,96,128]{2,1,0:T(8,128)(2,1)}), bf16[32,96,128]{2,1,0:T(8,128)(2,1)S(1)}, u32[]{:S(2)}, u32[]{:S(2)}) async-start(bf16[32,96,128]{2,1,0:T(8,128)(2,1)} %bitcast.6), calls=%async_computation.3 | async-start | bytes 1572864 | tf_op jit(solution)/shard_map/exchange_panels/all_to_all | solution.py:85
  85.5 16.8 %all-to-all-done.3 = bf16[32,96,128]{2,1,0:T(8,128)(2,1)S(1)} async-done(((bf16[32,96,128]{2,1,0:T(8,128)(2,1)}), bf16[32,96,128]{2,1,0:T(8,128)(2,1)S(1)}, u32[]{:S(2)}, u32[]{:S(2)}) %all-to-all-start.3) | async-done | bytes 786464 | tf_op jit(solution)/shard_map/exchange_panels/all_to_all | solution.py:85
  102.3 0.1 fusion.8
  102.4 0.1 constant_dynamic-slice_fusion
  102.5 0.1 copy.21
  102.6 0.0 copy-start
  102.7 9.1 %collective-permute-start = (bf16[2,192,768]{2,1,0:T(8,128)(2,1)S(1)}, bf16[2,192,768]{2,1,0:T(8,128)(2,1)S(1)}, u32[]{:S(2)}, u32[]{:S(2)}) collective-permute-start(bf16[2,192,768]{2,1,0:T(8,128)(2,1)S(1)} %pad_maximum_fusion.1), channel_id=1, source_target_pairs={{0,1},{1,0},{2,3},{3,2},{4,5},{5,4},{6,7},{7,6},{8,9},{9,8},{10,11... | collective-permute-start | bytes 1769480 | tf_op jit(solution)/shard_map/exchange_tp/ppermute | solution.py:97
  111.8 0.1 slice.28
  111.9 0.4 fusion.9
  112.3 1.1 collective-permute-done
  113.4 0.0 copy-done
  113.4 1.4 %fusion.2 = f32[2,256,512]{2,1,0:T(8,128)} fusion(f32[2,256,512]{2,1,0:T(8,128)S(1)} %fusion.9, f32[2,256,512]{2,1,0:T(8,128)S(1)} %copy-done, pred[2]{0:T(512)(128)(4,1)S(1)} %broadcast_compare_fusion, bf16[2,192,768]{2,1,0:T(8,128)(2,1)S(1)} %collective-permute-done), kind=kOutput, calls=%fused_computation.5 | convolution fusion | flops 101974016 | bytes 3735554 | tf_op jit(solution)/shard_map/sca,scb->sab/dot_general | solution.py:103
  (13 shorter events, 0.3 us)
Async XLA Ops:
  54.6 25.3 %all-to-all-start.2 = ((bf16[12,64,128]{2,1,0:T(8,128)(2,1)}), bf16[12,64,128]{2,1,0:T(8,128)(2,1)S(1)}, u32[]{:S(2)}, u32[]{:S(2)}) async-start(bf16[12,64,128]{2,1,0:T(8,128)(2,1)} %broadcast_in_dim.47), calls=%async_computation.2 | async-start | bytes 393216 | tf_op jit(solution)/shard_map/gather_z/all_to_all | solution.py:78
  81.5 20.8 %all-to-all-start.3 = ((bf16[32,96,128]{2,1,0:T(8,128)(2,1)}), bf16[32,96,128]{2,1,0:T(8,128)(2,1)S(1)}, u32[]{:S(2)}, u32[]{:S(2)}) async-start(bf16[32,96,128]{2,1,0:T(8,128)(2,1)} %bitcast.6), calls=%async_computation.3 | async-start | bytes 1572864 | tf_op jit(solution)/shard_map/exchange_panels/all_to_all | solution.py:85
  102.6 10.8 %copy-start = (f32[2,256,512]{2,1,0:T(8,128)S(1)}, f32[2,256,512]{2,1,0:T(8,128)}, u32[]{:S(2)}) copy-start(f32[2,256,512]{2,1,0:T(8,128)} %param.5) | copy-start | bytes 3145732
  102.7 10.7 %collective-permute-start = (bf16[2,192,768]{2,1,0:T(8,128)(2,1)S(1)}, bf16[2,192,768]{2,1,0:T(8,128)(2,1)S(1)}, u32[]{:S(2)}, u32[]{:S(2)}) collective-permute-start(bf16[2,192,768]{2,1,0:T(8,128)(2,1)S(1)} %pad_maximum_fusion.1), channel_id=1, source_target_pairs={{0,1},{1,0},{2,3},{3,2},{4,5},{5,4},{6,7},{7,6},{8,9},{9,8},{10,11... | collective-permute-start | bytes 1769480 | tf_op jit(solution)/shard_map/exchange_tp/ppermute | solution.py:97

commit v8 on v7

--- a/solution.py
+++ b/solution.py
@@ -19,20 +19,18 @@
 
 def pick_kernel(index_ref, table_ref, out_ref):
     def step(n, carry):
-        panels = [index_ref[n * PICKS + k] for k in range(PICKS)]
-        found = [[table_ref[z * PANELS + panel] for z in range(ZL)] for panel in panels]
+        found = [table_ref[index_ref[n * PICKS + k]] for k in range(PICKS)]
         for k in range(PICKS):
-            for z in range(ZL):
-                out_ref[n, k, z] = found[k][z]
+            out_ref[n * PICKS + k] = found[k]
         return carry
 
-    lax.fori_loop(0, PLANE, step, 0, unroll=4)
+    lax.fori_loop(0, PLANE, step, 0, unroll=8)
 
 
 def pick_pieces(index, table):
     return pl.pallas_call(
         pick_kernel,
-        out_shape=jax.ShapeDtypeStruct((PLANE, PICKS, ZL, SUB, LANES), table.dtype),
+        out_shape=jax.ShapeDtypeStruct((PLANE * PICKS, ZL * SUB, LANES), table.dtype),
         in_specs=[
             pl.BlockSpec(memory_space=pltpu.SMEM),
             pl.BlockSpec(memory_space=pltpu.VMEM),
@@ -78,7 +76,8 @@
         table = lax.all_to_all(
             jnp.broadcast_to(summed, (ZL * F, HERE * SUB, LANES)), ("zl", "fsdp"), 0, 0, tiled=True
         )
-    table = table.reshape(ZL * PANELS, SUB, LANES)
+    table = table.reshape(ZL, PANELS, SUB, LANES).transpose(1, 0, 2, 3)
+    table = table.reshape(PANELS, ZL * SUB, LANES)
     with jax.named_scope("pick"):
         pieces = pick_pieces(ends, table)
     with jax.named_scope("exchange_panels"):

time: 115 us -> 115 us (level)
  no operation moved by 1% of the time
where the time goes in v8:
time: 115 us
  blocking collectives  50.6 us (44%)
  waiting for transfers between devices  28.8 us (25%)
  starting transfers between devices  27.2 us (24%)
  other arithmetic  2.95 us (3%)
  matrix products  1.79 us (2%)
  local copies, waits for them, and re-layouts  1.69 us (1%)
  Pallas kernels  1.59 us (1%)
    all_to_all x1, blocking collectives, body(): lax.all_to_all(jnp.concatenate([columns, note], axis=2), ('yl', 'zl', 'x'...  34.5 us
    all_to_all x1, waiting for transfers between devices, body(): lax.all_to_all(pieces.reshape(PLANE, PICKS * ZL * SUB, LANES), ('yh', 'yl...  16.8 us
    all_to_all x1, blocking collectives, body(): lax.all_to_all(jnp.concatenate([blocks, note], axis=1), 'yh', 0, 0, tiled...  16.2 us
    all_to_all x1, starting transfers between devices, body(): lax.all_to_all(jnp.broadcast_to(summed, (ZL * F, HERE * SUB, LANES)), ('z...  14.2 us
    all_to_all x1, waiting for transfers between devices, body(): lax.all_to_all(jnp.broadcast_to(summed, (ZL * F, HERE * SUB, LANES)), ('z...  10.8 us
    ppermute x1, starting transfers between devices, body(): lax.ppermute(jnp.concatenate([row_half(1 - half), second], axis=2), 'tp',...  9.09 us
    all_to_all x1, starting transfers between devices, body(): lax.all_to_all(pieces.reshape(PLANE, PICKS * ZL * SUB, LANES), ('yh', 'yl...  3.91 us
  transfers between devices with their start and end apart: 3, of which 3 were waited for; matrix products, arithmetic and copies ran while one was open for 1% of the time, Pallas kernels for 0%

profile of v8, /device:TPU:1, one launch (start us, length us, event | category | flops | bytes accessed | tf_op | source)
XLA Modules:
  0.0 114.8 jit_solution(3731384591339363714)
XLA Ops:
  0.0 0.8 select_reduce_fusion.1
  0.8 0.1 fusion.7
  0.9 1.7 %pad_maximum_fusion = bf16[24,8,4224]{2,1,0:T(8,128)(2,1)S(1)} fusion(bf16[24,8,4096]{2,1,0:T(8,128)(2,1)} %bitcast.38, bf16[4224]{0:T(1024)(128)(2,1)S(1)} %fusion.5), kind=kLoop, calls=%fused_computation.1 | loop fusion | flops 3244032 | bytes 3203328 | tf_op jit(solution)/shard_map/exchange_near/concatenate | solution.py:56
  2.6 34.5 %all_to_all.20 = bf16[24,8,4224]{2,1,0:T(8,128)(2,1)S(1)} all-to-all(bf16[24,8,4224]{2,1,0:T(8,128)(2,1)S(1)} %pad_maximum_fusion), channel_id=1, replica_groups=mesh['yh'=4,'yl'=2,'zl'=3,'x'=4,'fsdp'=4,'tp'=2] {'yl','zl','x'}, dimensions={0} | all-to-all | bytes 3244032 | tf_op jit(solution)/shard_map/exchange_near/all_to_all | solution.py:55
  37.1 0.2 convert_reduce_fusion
  37.3 0.1 reshape.57
  37.4 0.1 copy.28
  37.5 0.1 convert_element_type.27
  37.7 16.2 %all_to_all.21 = f32[4,72,128]{2,1,0:T(8,128)S(1)} all-to-all(f32[4,72,128]{2,1,0:T(8,128)S(1)} %pad_maximum_fusion.2), channel_id=1, replica_groups=mesh['yh'=4,'yl'=2,'zl'=3,'x'=4,'fsdp'=4,'tp'=2] {'yh'}, dimensions={0} | all-to-all | bytes 294912 | tf_op jit(solution)/shard_map/exchange_far/all_to_all | solution.py:66
  53.9 0.7 broadcast_in_dim.47
  54.6 14.2 %all-to-all-start.2 = ((bf16[12,64,128]{2,1,0:T(8,128)(2,1)}), bf16[12,64,128]{2,1,0:T(8,128)(2,1)S(1)}, u32[]{:S(2)}, u32[]{:S(2)}) async-start(bf16[12,64,128]{2,1,0:T(8,128)(2,1)} %broadcast_in_dim.47), calls=%async_computation.2 | async-start | bytes 393216 | tf_op jit(solution)/shard_map/gather_z/all_to_all | solution.py:76
  68.8 0.1 convert_element_type.29
  69.0 0.1 max.12.index_ref
  69.0 10.8 %all-to-all-done.2 = bf16[12,64,128]{2,1,0:T(8,128)(2,1)S(1)} async-done(((bf16[12,64,128]{2,1,0:T(8,128)(2,1)}), bf16[12,64,128]{2,1,0:T(8,128)(2,1)S(1)}, u32[]{:S(2)}, u32[]{:S(2)}) %all-to-all-start.2) | async-done | bytes 196640 | tf_op jit(solution)/shard_map/gather_z/all_to_all | solution.py:76
  79.9 1.6 %pick.1 = bf16[128,24,128]{2,1,0:T(8,128)(2,1)} custom-call(s32[128]{0:T(128)S(1)} %max.12.index_ref, bf16[32,24,128]{2,1,0:T(8,128)(2,1)S(1)} %bitcast.34), custom_call_target="tpu_custom_call" | custom-call | bytes 2097152 | tf_op jit(solution)/shard_map/pick/pallas_call | solution.py:31
  81.5 3.9 %all-to-all-start.3 = ((bf16[32,96,128]{2,1,0:T(8,128)(2,1)}), bf16[32,96,128]{2,1,0:T(8,128)(2,1)S(1)}, u32[]{:S(2)}, u32[]{:S(2)}) async-start(bf16[32,96,128]{2,1,0:T(8,128)(2,1)} %bitcast.8), calls=%async_computation.3 | async-start | bytes 1572864 | tf_op jit(solution)/shard_map/exchange_panels/all_to_all | solution.py:84
  85.4 16.8 %all-to-all-done.3 = bf16[32,96,128]{2,1,0:T(8,128)(2,1)S(1)} async-done(((bf16[32,96,128]{2,1,0:T(8,128)(2,1)}), bf16[32,96,128]{2,1,0:T(8,128)(2,1)S(1)}, u32[]{:S(2)}, u32[]{:S(2)}) %all-to-all-start.3) | async-done | bytes 786464 | tf_op jit(solution)/shard_map/exchange_panels/all_to_all | solution.py:84
  102.3 0.1 fusion.8
  102.4 0.1 constant_dynamic-slice_fusion
  102.5 0.1 copy.24
  102.6 0.0 copy-start
  102.6 9.1 %collective-permute-start = (bf16[2,192,768]{2,1,0:T(8,128)(2,1)S(1)}, bf16[2,192,768]{2,1,0:T(8,128)(2,1)S(1)}, u32[]{:S(2)}, u32[]{:S(2)}) collective-permute-start(bf16[2,192,768]{2,1,0:T(8,128)(2,1)S(1)} %pad_maximum_fusion.1), channel_id=1, source_target_pairs={{0,1},{1,0},{2,3},{3,2},{4,5},{5,4},{6,7},{7,6},{8,9},{9,8},{10,11... | collective-permute-start | bytes 1769480 | tf_op jit(solution)/shard_map/exchange_tp/ppermute | solution.py:96
  111.7 0.1 slice.28
  111.9 0.4 fusion.9
  112.3 1.1 collective-permute-done
  113.4 0.0 copy-done
  113.4 1.4 %fusion.2 = f32[2,256,512]{2,1,0:T(8,128)} fusion(f32[2,256,512]{2,1,0:T(8,128)S(1)} %fusion.9, f32[2,256,512]{2,1,0:T(8,128)S(1)} %copy-done, pred[2]{0:T(512)(128)(4,1)S(1)} %broadcast_compare_fusion, bf16[2,192,768]{2,1,0:T(8,128)(2,1)S(1)} %collective-permute-done), kind=kOutput, calls=%fused_computation.5 | convolution fusion | flops 101974016 | bytes 3735554 | tf_op jit(solution)/shard_map/sca,scb->sab/dot_general | solution.py:102
  (14 shorter events, 0.3 us)
Async XLA Ops:
  54.6 25.3 %all-to-all-start.2 = ((bf16[12,64,128]{2,1,0:T(8,128)(2,1)}), bf16[12,64,128]{2,1,0:T(8,128)(2,1)S(1)}, u32[]{:S(2)}, u32[]{:S(2)}) async-start(bf16[12,64,128]{2,1,0:T(8,128)(2,1)} %broadcast_in_dim.47), calls=%async_computation.2 | async-start | bytes 393216 | tf_op jit(solution)/shard_map/gather_z/all_to_all | solution.py:76
  81.5 20.8 %all-to-all-start.3 = ((bf16[32,96,128]{2,1,0:T(8,128)(2,1)}), bf16[32,96,128]{2,1,0:T(8,128)(2,1)S(1)}, u32[]{:S(2)}, u32[]{:S(2)}) async-start(bf16[32,96,128]{2,1,0:T(8,128)(2,1)} %bitcast.8), calls=%async_computation.3 | async-start | bytes 1572864 | tf_op jit(solution)/shard_map/exchange_panels/all_to_all | solution.py:84
  102.6 10.8 %copy-start = (f32[2,256,512]{2,1,0:T(8,128)S(1)}, f32[2,256,512]{2,1,0:T(8,128)}, u32[]{:S(2)}) copy-start(f32[2,256,512]{2,1,0:T(8,128)} %param.5) | copy-start | bytes 3145732
  102.6 10.7 %collective-permute-start = (bf16[2,192,768]{2,1,0:T(8,128)(2,1)S(1)}, bf16[2,192,768]{2,1,0:T(8,128)(2,1)S(1)}, u32[]{:S(2)}, u32[]{:S(2)}) collective-permute-start(bf16[2,192,768]{2,1,0:T(8,128)(2,1)S(1)} %pad_maximum_fusion.1), channel_id=1, source_target_pairs={{0,1},{1,0},{2,3},{3,2},{4,5},{5,4},{6,7},{7,6},{8,9},{9,8},{10,11... | collective-permute-start | bytes 1769480 | tf_op jit(solution)/shard_map/exchange_tp/ppermute | solution.py:96

commit v9 on v7

--- a/solution.py
+++ b/solution.py
@@ -51,14 +51,16 @@
     own = [jnp.where(turn == 2 * place + s, slot_panels, 0).sum(0) for s in range(2)]
     own = jnp.concatenate(own)
     columns = grads[0].T.reshape(NEAR, width // NEAR, rows)
-    note = jnp.pad(own.astype(grads.dtype), (0, LANES - PICKS))
-    note = jnp.broadcast_to(note, (NEAR, width // NEAR, LANES))
+    note = slot_panels.T.astype(grads.dtype)
+    note = jnp.pad(note, ((0, SUB - 2), (0, LANES - F * 2)))
+    note = jnp.broadcast_to(note, (NEAR, SUB, LANES))
     with jax.named_scope("exchange_near"):
         came = lax.all_to_all(
             jnp.concatenate([columns, note], axis=2), ("yl", "zl", "x"), 0, 0, tiled=True
         )
     near_sum = came[:, :, :rows].astype(jnp.float32).sum(0)
-    near_ends = came[:, 0, rows : rows + PICKS].astype(jnp.float32)
+    near_ends = came[:, :2, rows : rows + F * 2].astype(jnp.float32)
+    near_ends = lax.dynamic_slice_in_dim(near_ends, 2 * place, 2, axis=2).transpose(0, 2, 1)
 
     blocks = near_sum.reshape(SUB, HERE, YH, LANES).transpose(2, 1, 0, 3)
     blocks = blocks.reshape(YH, HERE * SUB, LANES)

time: 115 us -> 118 us (1.026)
  blocking collectives: 50.6 us -> 16.6 us
  waiting for transfers between devices: 28.8 us -> 52.3 us
  starting transfers between devices: 27.2 us -> 37.5 us
  local copies, waits for them, and re-layouts: 1.66 us -> 3.02 us
  other arithmetic: 2.95 us -> 4.15 us
    all_to_all x1 -> x0, blocking collectives: 34.5 us -> none  [body(): lax.all_to_all(jnp.concatenate([columns, note], axis=2), ('yl', 'zl', 'x'...]
    all_to_all x0 -> x1, waiting for transfers between devices: none -> 23.1 us  [body(): lax.all_to_all(jnp.concatenate([columns, note], axis=2), ('yl', 'zl', 'x'...]
    all_to_all x0 -> x1, starting transfers between devices: none -> 9.73 us  [body(): lax.all_to_all(jnp.concatenate([columns, note], axis=2), ('yl', 'zl', 'x'...]
    concatenate x2 -> x1, other arithmetic: 1.69 us -> 2.74 us  [body(): jnp.concatenate([columns, note], axis=2)]
  transfers between devices with their start and end apart: 3 -> 4, of which waited for: 3 -> 4; matrix products, arithmetic and copies ran while one was open for 1% -> 1% of each run, Pallas kernels for 0% -> 0%
where the time goes in v9:
time: 118 us; the launch traced here: 117 us
  waiting for transfers between devices  52.3 us (44%)
  starting transfers between devices  37.5 us (32%)
  blocking collectives  16.6 us (14%)
  other arithmetic  4.15 us (4%)
  local copies, waits for them, and re-layouts  3.02 us (3%)
  matrix products  1.79 us (2%)
  Pallas kernels  1.67 us (1%)
    all_to_all x1, waiting for transfers between devices, body(): lax.all_to_all(jnp.concatenate([columns, note], axis=2), ('yl', 'zl', 'x'...  23.1 us
    all_to_all x1, waiting for transfers between devices, body(): lax.all_to_all(pieces.reshape(PLANE, PICKS * ZL * SUB, LANES), ('yh', 'yl...  17.3 us
    all_to_all x1, blocking collectives, body(): lax.all_to_all(jnp.concatenate([blocks, note], axis=1), 'yh', 0, 0, tiled...  16.6 us
    all_to_all x1, starting transfers between devices, body(): lax.all_to_all(jnp.broadcast_to(summed, (ZL * F, HERE * SUB, LANES)), ('z...  14.2 us
    all_to_all x1, waiting for transfers between devices, body(): lax.all_to_all(jnp.broadcast_to(summed, (ZL * F, HERE * SUB, LANES)), ('z...  10.8 us
    all_to_all x1, starting transfers between devices, body(): lax.all_to_all(jnp.concatenate([columns, note], axis=2), ('yl', 'zl', 'x'...  9.73 us
    ppermute x1, starting transfers between devices, body(): lax.ppermute(jnp.concatenate([row_half(1 - half), second], axis=2), 'tp',...  8.71 us
    all_to_all x1, starting transfers between devices, body(): lax.all_to_all(pieces.reshape(PLANE, PICKS * ZL * SUB, LANES), ('yh', 'yl...  4.84 us
  transfers between devices with their start and end apart: 4, of which 4 were waited for; matrix products, arithmetic and copies ran while one was open for 1% of the time, Pallas kernels for 0%

profile of v9, /device:TPU:1, one launch (start us, length us, event | category | flops | bytes accessed | tf_op | source)
XLA Modules:
  0.0 117.2 jit_solution(17779665900376583707)
XLA Ops:
  0.0 0.9 select_reduce_fusion.1
  0.9 2.7 %pad_maximum_fusion = bf16[24,8,4224]{2,1,0:T(8,128)(2,1)} fusion(bf16[24,8,128]{2,1,0:T(8,128)(2,1)S(1)} %broadcast_in_dim.45, bf16[24,8,4096]{2,1,0:T(8,128)(2,1)} %bitcast.39), kind=kLoop, calls=%fused_computation.1 | loop fusion | flops 3244032 | bytes 3244032 | tf_op jit(solution)/shard_map/exchange_near/concatenate | solution.py:59
  3.7 9.7 %all-to-all-start = ((bf16[24,8,4224]{2,1,0:T(8,128)(2,1)}), bf16[24,8,4224]{2,1,0:T(8,128)(2,1)S(1)}, u32[]{:S(2)}, u32[]{:S(2)}) async-start(bf16[24,8,4224]{2,1,0:T(8,128)(2,1)} %pad_maximum_fusion), calls=%async_computation | async-start | bytes 3244032 | tf_op jit(solution)/shard_map/exchange_near/all_to_all | solution.py:58
  13.4 23.1 %all-to-all-done = bf16[24,8,4224]{2,1,0:T(8,128)(2,1)S(1)} async-done(((bf16[24,8,4224]{2,1,0:T(8,128)(2,1)}), bf16[24,8,4224]{2,1,0:T(8,128)(2,1)S(1)}, u32[]{:S(2)}, u32[]{:S(2)}) %all-to-all-start) | async-done | bytes 1622048 | tf_op jit(solution)/shard_map/exchange_near/all_to_all | solution.py:58
  36.6 0.1 convert_bitcast_fusion
  36.6 0.3 copy.23
  36.9 0.1 reshape.55
  37.0 0.2 convert_reduce_fusion
  37.3 0.6 copy.28
  37.9 0.6 copy.27
  38.5 0.1 copy.31
  38.6 16.6 %all_to_all.20 = f32[4,72,128]{2,1,0:T(8,128)S(1)} all-to-all(f32[4,72,128]{2,1,0:T(8,128)S(1)} %pad_maximum_fusion.2), channel_id=1, replica_groups=mesh['yh'=4,'yl'=2,'zl'=3,'x'=4,'fsdp'=4,'tp'=2] {'yh'}, dimensions={0} | all-to-all | bytes 294912 | tf_op jit(solution)/shard_map/exchange_far/all_to_all | solution.py:70
  55.2 0.7 broadcast_in_dim.47
  55.9 14.2 %all-to-all-start.2 = ((bf16[12,64,128]{2,1,0:T(8,128)(2,1)}), bf16[12,64,128]{2,1,0:T(8,128)(2,1)S(1)}, u32[]{:S(2)}, u32[]{:S(2)}) async-start(bf16[12,64,128]{2,1,0:T(8,128)(2,1)} %broadcast_in_dim.47), calls=%async_computation.2 | async-start | bytes 393216 | tf_op jit(solution)/shard_map/gather_z/all_to_all | solution.py:80
  70.2 0.1 convert_element_type.31
  70.3 0.1 max.12.index_ref
  70.4 10.8 %all-to-all-done.2 = bf16[12,64,128]{2,1,0:T(8,128)(2,1)S(1)} async-done(((bf16[12,64,128]{2,1,0:T(8,128)(2,1)}), bf16[12,64,128]{2,1,0:T(8,128)(2,1)S(1)}, u32[]{:S(2)}, u32[]{:S(2)}) %all-to-all-start.2) | async-done | bytes 196640 | tf_op jit(solution)/shard_map/gather_z/all_to_all | solution.py:80
  81.2 1.7 %pick.1 = bf16[32,4,3,8,128]{4,3,2,1,0:T(8,128)(2,1)} custom-call(s32[128]{0:T(128)S(1)} %max.12.index_ref, bf16[96,8,128]{2,1,0:T(8,128)(2,1)S(1)} %bitcast.34), custom_call_target="tpu_custom_call" | custom-call | bytes 2097152 | tf_op jit(solution)/shard_map/pick/pallas_call | solution.py:33
  82.9 4.8 %all-to-all-start.3 = ((bf16[32,96,128]{2,1,0:T(8,128)(2,1)}), bf16[32,96,128]{2,1,0:T(8,128)(2,1)S(1)}, u32[]{:S(2)}, u32[]{:S(2)}) async-start(bf16[32,96,128]{2,1,0:T(8,128)(2,1)} %bitcast.9), calls=%async_computation.3 | async-start | bytes 1572864 | tf_op jit(solution)/shard_map/exchange_panels/all_to_all | solution.py:87
  87.7 17.3 %all-to-all-done.3 = bf16[32,96,128]{2,1,0:T(8,128)(2,1)S(1)} async-done(((bf16[32,96,128]{2,1,0:T(8,128)(2,1)}), bf16[32,96,128]{2,1,0:T(8,128)(2,1)S(1)}, u32[]{:S(2)}, u32[]{:S(2)}) %all-to-all-start.3) | async-done | bytes 786464 | tf_op jit(solution)/shard_map/exchange_panels/all_to_all | solution.py:87
  105.0 0.1 fusion.6
  105.2 0.1 constant_dynamic-slice_fusion
  105.3 0.1 copy.29
  105.4 0.0 copy-start
  105.4 8.7 %collective-permute-start = (bf16[2,192,768]{2,1,0:T(8,128)(2,1)S(1)}, bf16[2,192,768]{2,1,0:T(8,128)(2,1)S(1)}, u32[]{:S(2)}, u32[]{:S(2)}) collective-permute-start(bf16[2,192,768]{2,1,0:T(8,128)(2,1)S(1)} %pad_maximum_fusion.1), channel_id=1, source_target_pairs={{0,1},{1,0},{2,3},{3,2},{4,5},{5,4},{6,7},{7,6},{8,9},{9,8},{10,11... | collective-permute-start | bytes 1769480 | tf_op jit(solution)/shard_map/exchange_tp/ppermute | solution.py:99
  114.1 0.1 pad_add_fusion
  114.2 0.1 slice.28
  114.4 0.4 fusion.7
  114.7 1.0 collective-permute-done
  115.8 0.0 copy-done
  115.8 1.4 %fusion.2 = f32[2,256,512]{2,1,0:T(8,128)} fusion(f32[2,256,512]{2,1,0:T(8,128)S(1)} %fusion.7, f32[2,256,512]{2,1,0:T(8,128)S(1)} %copy-done, pred[2]{0:T(512)(128)(4,1)S(1)} %broadcast_compare_fusion, bf16[2,192,768]{2,1,0:T(8,128)(2,1)S(1)} %collective-permute-done), kind=kOutput, calls=%fused_computation.5 | convolution fusion | flops 101974016 | bytes 3735554 | tf_op jit(solution)/shard_map/sca,scb->sab/dot_general | solution.py:105
  (14 shorter events, 0.2 us)
Async XLA Ops:
  3.7 32.9 %all-to-all-start = ((bf16[24,8,4224]{2,1,0:T(8,128)(2,1)}), bf16[24,8,4224]{2,1,0:T(8,128)(2,1)S(1)}, u32[]{:S(2)}, u32[]{:S(2)}) async-start(bf16[24,8,4224]{2,1,0:T(8,128)(2,1)} %pad_maximum_fusion), calls=%async_computation | async-start | bytes 3244032 | tf_op jit(solution)/shard_map/exchange_near/all_to_all | solution.py:58
  55.9 25.3 %all-to-all-start.2 = ((bf16[12,64,128]{2,1,0:T(8,128)(2,1)}), bf16[12,64,128]{2,1,0:T(8,128)(2,1)S(1)}, u32[]{:S(2)}, u32[]{:S(2)}) async-start(bf16[12,64,128]{2,1,0:T(8,128)(2,1)} %broadcast_in_dim.47), calls=%async_computation.2 | async-start | bytes 393216 | tf_op jit(solution)/shard_map/gather_z/all_to_all | solution.py:80
  82.9 22.2 %all-to-all-start.3 = ((bf16[32,96,128]{2,1,0:T(8,128)(2,1)}), bf16[32,96,128]{2,1,0:T(8,128)(2,1)S(1)}, u32[]{:S(2)}, u32[]{:S(2)}) async-start(bf16[32,96,128]{2,1,0:T(8,128)(2,1)} %bitcast.9), calls=%async_computation.3 | async-start | bytes 1572864 | tf_op jit(solution)/shard_map/exchange_panels/all_to_all | solution.py:87
  105.4 10.4 %copy-start = (f32[2,256,512]{2,1,0:T(8,128)S(1)}, f32[2,256,512]{2,1,0:T(8,128)}, u32[]{:S(2)}) copy-start(f32[2,256,512]{2,1,0:T(8,128)} %param.5) | copy-start | bytes 3145732
  105.4 10.3 %collective-permute-start = (bf16[2,192,768]{2,1,0:T(8,128)(2,1)S(1)}, bf16[2,192,768]{2,1,0:T(8,128)(2,1)S(1)}, u32[]{:S(2)}, u32[]{:S(2)}) collective-permute-start(bf16[2,192,768]{2,1,0:T(8,128)(2,1)S(1)} %pad_maximum_fusion.1), channel_id=1, source_target_pairs={{0,1},{1,0},{2,3},{3,2},{4,5},{5,4},{6,7},{7,6},{8,9},{9,8},{10,11... | collective-permute-start | bytes 1769480 | tf_op jit(solution)/shard_map/exchange_tp/ppermute | solution.py:99
